TPU v7x, 256 devices: a whole 4x4x8 slice. The times are simulated.
256 devices in a mesh: grp: 16 (over y, x), blk: 16 (over z, core).
Axes of the slice: x: 4, y: 4, z: 8, core: 2. Of those that a mesh axis runs over, the one named last changes fastest.
Arguments:
- queries: bfloat16 [32768, 1024], P(('grp', 'blk')), may hold values from -8 to 8
- key_rows: bfloat16 [32768, 128], P(('grp', 'blk')), may hold values from -8 to 8
- values: bfloat16 [32768, 128], P(('grp', 'blk')), may hold values from -6 to 6
- out_grad: bfloat16 [32768, 1024], P(('grp', 'blk')), may hold values from -6 to 6
- span_order: int32 [16], replicated, may hold values from 0 to 15, each once
Outputs:
- attended: bfloat16 [32768, 1024], P(('grp', 'blk'))
- grad_queries: bfloat16 [32768, 1024], P(('grp', 'blk'))
- grad_keys: bfloat16 [32768, 128], P(('grp', 'blk'))
- grad_values: bfloat16 [32768, 128], P(('grp', 'blk'))
Inputs may be any that keep to these rules, and one draw needn't show every extreme that they name: `span_order`: a permutation of 0 to 15.
All inputs are finite; a program needn't handle non-finite values.
Results may differ from a plain program's by a relative error of at most 0.015.
Values may be sent and summed in bfloat16 or wider, within the bound.
A program may use at most 64 MiB of HBM per device.

v0:
```python
import math

import jax
import jax.numpy as jnp
from jax import lax
from jax.sharding import PartitionSpec as P

HEAD = 128


NEG_FILL = -1e30


def from_behind(block, axis, distance):
    devices = range(lax.axis_size(axis))
    route = [((i - distance) % len(devices), i) for i in devices]
    return lax.ppermute(block, axis, route)


def positions(span_order, grp_ids, blk_id, row_count, grp_count, blk_count):
    halfway = grp_count // 2
    columns = jnp.arange(blk_count, dtype=jnp.int32)
    lead_part = jnp.sum(jnp.where(columns == blk_id, span_order, 0))
    section = jnp.where(grp_ids < halfway, lead_part, 2 * blk_count - 1 - lead_part)
    inside = jnp.arange(row_count, dtype=jnp.int32)
    places = (
        section[:, None] * (halfway * row_count)
        + (grp_ids % halfway)[:, None] * row_count
        + inside[None, :]
    )
    return places.reshape(-1)


def masked_scores(query_head, key_head, query_pos, key_pos, factor):
    raw_scores = (
        jnp.einsum("qd,kd->qk", query_head, key_head, preferred_element_type=jnp.float32) * factor
    )
    visible = key_pos[None, :] <= query_pos[:, None]
    return (jnp.where(visible, raw_scores, NEG_FILL), visible)


def attend(query_rows, grad_rows, query_pos, kv_sets, key_pos_sets, sum_hook):
    head_dim = HEAD
    head_count = query_rows.shape[1] // head_dim
    query_count = query_rows.shape[0]
    factor = 1.0 / math.sqrt(head_dim)
    set_count = len(kv_sets)
    key_list = [member[:, :head_dim] for member in kv_sets]
    value_list = [member[:, head_dim:] for member in kv_sets]

    def column_of(matrix, head_idx):
        return lax.dynamic_slice_in_dim(matrix, head_idx * head_dim, head_dim, 1)

    maxima = jnp.zeros((query_count, head_count), jnp.float32)

    def forward_step(head_idx, running):
        blended, totals, found = running
        query_head = column_of(query_rows, head_idx)
        score_sets = [
            masked_scores(query_head, key_list[member], query_pos, key_pos_sets[member], factor)
            for member in range(set_count)
        ]
        row_top = jnp.full((query_count, 1), NEG_FILL, jnp.float32)
        for scores, visible in score_sets:
            row_top = jnp.maximum(row_top, jnp.max(scores, axis=1, keepdims=True))
        found = lax.dynamic_update_slice_in_dim(found, row_top, head_idx, 1)
        summed = jnp.zeros((query_count, head_dim), jnp.float32)
        row_total = jnp.zeros((query_count, 1), jnp.float32)
        for member in range(set_count):
            scores, visible = score_sets[member]
            weights = jnp.where(visible, jnp.exp(scores - row_top), 0.0)
            row_total = row_total + jnp.sum(weights, axis=1, keepdims=True)
            summed = summed + jnp.dot(
                weights.astype(jnp.bfloat16), value_list[member], preferred_element_type=jnp.float32
            )
        blended = lax.dynamic_update_slice_in_dim(blended, summed, head_idx * head_dim, 1)
        totals = lax.dynamic_update_slice_in_dim(totals, row_total, head_idx, 1)
        return (blended, totals, found)

    start_state = (
        jnp.zeros((query_count, head_count * head_dim), jnp.float32),
        jnp.zeros((query_count, head_count), jnp.float32),
        maxima,
    )
    blended, totals, maxima = lax.fori_loop(0, head_count, forward_step, start_state)
    blended, totals = sum_hook(blended, totals)
    out_heads = lax.optimization_barrier(
        (blended.reshape(query_count, head_count, head_dim) / totals[:, :, None]).astype(
            jnp.bfloat16
        )
    )
    grad_heads = grad_rows.reshape(query_count, head_count, head_dim)
    deltas = jnp.sum(grad_heads.astype(jnp.float32) * out_heads.astype(jnp.float32), axis=2)
    out_rows = out_heads.reshape(query_count, head_count * head_dim)

    def backward_step(head_idx, running):
        query_grad = running[0]
        query_head = column_of(query_rows, head_idx)
        grad_head = column_of(grad_rows, head_idx)
        row_top = lax.dynamic_slice_in_dim(maxima, head_idx, 1, 1)
        row_total = lax.dynamic_slice_in_dim(totals, head_idx, 1, 1)
        row_delta = lax.dynamic_slice_in_dim(deltas, head_idx, 1, 1)
        head_grad = jnp.zeros((query_count, head_dim), jnp.float32)
        updated = []
        for member in range(set_count):
            scores, visible = masked_scores(
                query_head, key_list[member], query_pos, key_pos_sets[member], factor
            )
            normed = jnp.where(visible, jnp.exp(scores - row_top), 0.0) / row_total
            value_grad = jnp.einsum(
                "qk,qd->kd",
                normed.astype(jnp.bfloat16),
                grad_head,
                preferred_element_type=jnp.float32,
            )
            prob_grad = jnp.einsum(
                "qd,kd->qk", grad_head, value_list[member], preferred_element_type=jnp.float32
            )
            score_grad = (normed * (prob_grad - row_delta)).astype(jnp.bfloat16)
            head_grad = head_grad + jnp.dot(
                score_grad, key_list[member], preferred_element_type=jnp.float32
            )
            key_grad = jnp.einsum(
                "qk,qd->kd", score_grad, query_head, preferred_element_type=jnp.float32
            )
            updated.append(running[1 + member] + jnp.concatenate([key_grad, value_grad], axis=1))
        query_grad = lax.dynamic_update_slice_in_dim(query_grad, head_grad, head_idx * head_dim, 1)
        return (query_grad,) + tuple(updated)

    start_grads = (jnp.zeros((query_count, head_count * head_dim), jnp.float32),) + tuple(
        (jnp.zeros((member.shape[0], 2 * head_dim), jnp.float32) for member in kv_sets)
    )
    finished = lax.fori_loop(0, head_count, backward_step, start_grads)
    query_grad = finished[0] * factor
    kv_grads = tuple(
        (
            jnp.concatenate([member[:, :head_dim] * factor, member[:, head_dim:]], axis=1)
            for member in finished[1:]
        )
    )
    return (out_rows, query_grad, kv_grads)


def body(queries, key_rows, values, out_grad, span_order):
    row_count = queries.shape[0]
    grp_count = lax.axis_size("grp")
    blk_count = lax.axis_size("blk")
    grp_idx = lax.axis_index("grp")
    blk_idx = lax.axis_index("blk")
    paired = jnp.concatenate([key_rows, values], axis=1)
    from_lower = from_behind(paired, "blk", 1)
    from_upper = from_behind(paired, "blk", -1)
    nearby = [(blk_idx + blk_count - 1) % blk_count, blk_idx, (blk_idx + 1) % blk_count]
    every_grp = jnp.arange(grp_count, dtype=jnp.int32)
    own_grp = jnp.reshape(grp_idx, (1,))
    gathered = (
        lax.all_gather(from_lower, "grp", axis=0, tiled=True),
        lax.all_gather(paired, "grp", axis=0, tiled=True),
        lax.all_gather(from_upper, "grp", axis=0, tiled=True),
    )
    query_pos = positions(span_order, own_grp, blk_idx, row_count, grp_count, blk_count)
    key_pos_sets = [
        positions(span_order, every_grp, neighbor, row_count, grp_count, blk_count)
        for neighbor in nearby
    ]
    out_own, query_own, grads_wide = attend(
        queries,
        out_grad,
        query_pos,
        [gathered[0], gathered[1], gathered[2]],
        key_pos_sets,
        lambda blended, totals: (blended, totals),
    )
    kv_grads = (
        lax.psum_scatter(
            grads_wide[0].astype(jnp.bfloat16), "grp", scatter_dimension=0, tiled=True
        ).astype(jnp.float32),
        lax.psum_scatter(
            grads_wide[1].astype(jnp.bfloat16), "grp", scatter_dimension=0, tiled=True
        ).astype(jnp.float32),
        lax.psum_scatter(
            grads_wide[2].astype(jnp.bfloat16), "grp", scatter_dimension=0, tiled=True
        ).astype(jnp.float32),
    )
    to_lower = from_behind(kv_grads[0].astype(jnp.bfloat16), "blk", -1).astype(jnp.float32)
    to_upper = from_behind(kv_grads[2].astype(jnp.bfloat16), "blk", 1).astype(jnp.float32)
    kv_total = kv_grads[1] + to_lower + to_upper
    return (
        out_own,
        query_own.astype(jnp.bfloat16),
        kv_total[:, :HEAD].astype(jnp.bfloat16),
        kv_total[:, HEAD:].astype(jnp.bfloat16),
    )


def solution(mesh):
    return jax.shard_map(
        body,
        mesh=mesh,
        in_specs=(
            P(("grp", "blk"), None),
            P(("grp", "blk"), None),
            P(("grp", "blk"), None),
            P(("grp", "blk"), None),
            P(),
        ),
        out_specs=(
            P(("grp", "blk"), None),
            P(("grp", "blk"), None),
            P(("grp", "blk"), None),
            P(("grp", "blk"), None),
        ),
        check_vma=False,
    )
```

profile of v0, /device:TPU:4, one launch (start us, length us, event | category | flops | bytes accessed | tf_op | source)
XLA Modules:
  0.0 583.4 jit_solution(14342851687694619981)
XLA Ops:
  9.4 5.3 collective-permute-start.1
  14.8 2.2 collective-permute-done.1
  17.7 5.1 collective-permute-done
  31.3 29.8 %all-gather.6.cloned.1.call-done = bf16[2048,256]{1,0:T(8,128)(2,1)} async-done(((bf16[128,256]{1,0:T(8,128)(2,1)}), bf16[2048,256]{1,0:T(8,128)(2,1)}) %all-gather.6.cloned.1.call-update) | async-done | bytes 1048592 | tf_op jit(solution)/shard_map/all_gather | solution.py:158
  61.1 2.1 fusion.121
  63.2 47.4 %all-gather.8.cloned.1.call-done = bf16[2048,256]{1,0:T(8,128)(2,1)} async-done(((bf16[128,256]{1,0:T(8,128)(2,1)}), bf16[2048,256]{1,0:T(8,128)(2,1)}) %all-gather.8.cloned.1.call-update) | async-done | bytes 1048592 | tf_op jit(solution)/shard_map/all_gather | solution.py:159
  110.6 2.1 fusion.120
  112.7 48.0 %all-gather.4.cloned.1.call-done = bf16[2048,256]{1,0:T(8,128)(2,1)} async-done(((bf16[128,256]{1,0:T(8,128)(2,1)}), bf16[2048,256]{1,0:T(8,128)(2,1)}) %all-gather.4.cloned.1.call-update) | async-done | bytes 1048592 | tf_op jit(solution)/shard_map/all_gather | solution.py:157
  160.7 2.3 fusion.122
  163.8 53.3 %while.38 = (s32[]{:T(128)}, f32[128,1024]{1,0:T(8,128)}, f32[128,8]{0,1:T(8,128)S(1)}, f32[128,8]{0,1:T(8,128)S(1)}, bf16[128,1024]{1,0:T(8,128)(2,1)}, /*index...) while((s32[]{:T(128)}, f32[128,1024]{1,0:T(8,128)}, ...), condition=%wide.region_10.11_spmd.clone, body=%wide.region_3.10_spmd.clone.sunk | while | flops 412129280 | bytes 21511728 | solution.py:85
  217.2 2.0 copy.24
  223.4 106.5 %while.39 = (s32[]{:T(128)}, f32[128,1024]{1,0:T(8,128)}, f32[2048,256]{0,1:T(8,128)}, f32[2048,256]{0,1:T(8,128)}, f32[2048,256]{0,1:T(8,128)S(1)}, /*index=5*/...) while((s32[]{:T(128)}, f32[128,1024]{1,0:T(8,128)}, ...), condition=%wide.region_13.14_spmd.clone, body=%wide.region_12.13_spmd.clone.sunk | while | flops 1019254912 | bytes 87812376 | solution.py:133
  223.7 1.6 fusion.255
  230.6 1.5 maximum_add_fusion.5
  237.0 1.6 fusion.255
  243.9 1.5 maximum_add_fusion.5
  250.3 1.6 fusion.255
  257.2 1.5 maximum_add_fusion.5
  263.6 1.6 fusion.255
  270.5 1.5 maximum_add_fusion.5
  276.9 1.6 fusion.255
  283.8 1.5 maximum_add_fusion.5
  290.2 1.6 fusion.255
  303.6 1.6 fusion.255
  316.9 1.6 fusion.255
  323.7 1.5 maximum_add_fusion.5
  329.9 1.9 copy.22
  335.7 1.8 copy.20
  341.5 1.8 copy.18
  347.1 66.1 %reduce-scatter.8.cloned.1.call-done = bf16[128,256]{1,0:T(8,128)(2,1)} async-done(((bf16[2048,256]{1,0:T(8,128)(2,1)}), bf16[128,256]{1,0:T(8,128)(2,1)}) %reduce-scatter.8.cloned.1.call-update) | async-done | bytes 65552 | tf_op jit(solution)/shard_map/reduce_scatter | solution.py:181
  413.2 81.1 %reduce-scatter.6.cloned.1.call-done = bf16[128,256]{1,0:T(8,128)(2,1)} async-done(((bf16[2048,256]{1,0:T(8,128)(2,1)}), bf16[128,256]{1,0:T(8,128)(2,1)}) %reduce-scatter.6.cloned.1.call-update) | async-done | bytes 65552 | tf_op jit(solution)/shard_map/reduce_scatter | solution.py:175
  496.4 78.7 %reduce-scatter.4.cloned.1.call-done = bf16[128,256]{1,0:T(8,128)(2,1)} async-done(((bf16[2048,256]{1,0:T(8,128)(2,1)}), bf16[128,256]{1,0:T(8,128)(2,1)}) %reduce-scatter.4.cloned.1.call-update) | async-done | bytes 65552 | tf_op jit(solution)/shard_map/reduce_scatter | solution.py:178
  (564 shorter events, 164.7 us)
Async XLA Ops:
  7.2 53.9 %all-gather.6.cloned.1.call-start = ((), (), s32[]{:S(2)}) async-start(), calls=%async_computation.4 | async-start | bytes 1114112 | tf_op jit(solution)/shard_map/all_gather | solution.py:158
  9.4 101.2 %all-gather.8.cloned.1.call-start = ((), (), s32[]{:S(2)}) async-start(), calls=%async_computation.5 | async-start | bytes 1114112 | tf_op jit(solution)/shard_map/all_gather | solution.py:159
  9.4 7.5 %collective-permute-start.1 = (bf16[128,256]{1,0:T(8,128)(2,1)}, bf16[128,256]{1,0:T(8,128)(2,1)S(1)}, u32[]{:S(2)}, u32[]{:S(2)}) collective-permute-start(bf16[128,256]{1,0:T(8,128)(2,1)} %copy-done.19), channel_id=1, source_target_pairs={{1,0},{2,1},{3,2},{4,3},{5,4},{6,5},{7,6},{8,7},{9,8},{10,9},{11,1... | collective-permute-start | bytes 196616 | tf_op jit(solution)/shard_map/ppermute | solution.py:17
  17.6 143.0 %all-gather.4.cloned.1.call-start = ((), (), s32[]{:S(2)}) async-start(), calls=%async_computation.3 | async-start | bytes 1114112 | tf_op jit(solution)/shard_map/all_gather | solution.py:157
  17.7 5.1 collective-permute-start
  23.4 389.8 %reduce-scatter.8.cloned.1.call-start = ((), (), s32[]{:S(2)}) async-start(), calls=%async_computation.8 | async-start | bytes 1114112 | tf_op jit(solution)/shard_map/reduce_scatter | solution.py:181
  163.8 2.5 copy-start.6
  170.5 2.5 copy-start.6
  177.2 2.5 copy-start.6
  183.8 2.5 copy-start.6
  190.5 2.5 copy-start.6
  193.0 2.0 copy-start.12
  197.2 2.5 copy-start.6
  203.8 2.5 copy-start.6
  210.5 2.5 copy-start.6
  217.2 6.3 %copy-start.14 = (bf16[128,1024]{1,0:T(8,128)(2,1)S(1)}, bf16[128,1024]{1,0:T(8,128)(2,1)}, u32[]{:S(2)}) copy-start(bf16[128,1024]{1,0:T(8,128)(2,1)} %param.12) | copy-start | bytes 786436
  228.3 2.2 copy-start.3
  241.6 2.2 copy-start.3
  255.0 2.2 copy-start.3
  268.3 2.2 copy-start.3
  281.6 2.2 copy-start.3
  294.9 2.2 copy-start.3
  308.2 2.2 copy-start.3
  321.5 2.2 copy-start.3
  333.0 2.6 copy-start.5
  335.6 158.7 %reduce-scatter.6.cloned.1.call-start = ((), (), s32[]{:S(2)}) async-start(), calls=%async_computation.7 | async-start | bytes 1114112 | tf_op jit(solution)/shard_map/reduce_scatter | solution.py:175
  338.8 2.7 copy-start.2
  341.4 233.6 %reduce-scatter.4.cloned.1.call-start = ((), (), s32[]{:S(2)}) async-start(), calls=%async_computation.6 | async-start | bytes 1114112 | tf_op jit(solution)/shard_map/reduce_scatter | solution.py:178
  344.6 150.3 %copy-start.18 = (f32[128,1024]{1,0:T(8,128)S(1)}, f32[128,1024]{1,0:T(8,128)}, u32[]{:S(2)}) copy-start(f32[128,1024]{1,0:T(8,128)} %get-tuple-element.575) | copy-start | bytes 1572868
  346.0 149.6 %copy-start.17 = (bf16[128,8,128]{2,1,0:T(8,128)(2,1)S(1)}, bf16[128,8,128]{2,1,0:T(8,128)(2,1)}, u32[]{:S(2)}) copy-start(bf16[128,8,128]{2,1,0:T(8,128)(2,1)} %copy-done.16) | copy-start | bytes 786436
  413.2 161.8 %collective-permute-start.3 = (bf16[128,256]{1,0:T(8,128)(2,1)}, bf16[128,256]{1,0:T(8,128)(2,1)S(1)}, u32[]{:S(2)}, u32[]{:S(2)}) collective-permute-start(bf16[128,256]{1,0:T(8,128)(2,1)} %reduce-scatter.8.cloned.1.call-done), channel_id=1, source_target_pairs={{15,0},{0,1},{1,2},{2,3},{3,4},{4,5},{5,6},{6,7},{7,8},{8,9},{9,10... | collective-permute-start | bytes 196616 | tf_op jit(solution)/shard_map/ppermute | solution.py:17
  494.3 80.8 %collective-permute-start.2 = (bf16[128,256]{1,0:T(8,128)(2,1)}, bf16[128,256]{1,0:T(8,128)(2,1)S(1)}, u32[]{:S(2)}, u32[]{:S(2)}) collective-permute-start(bf16[128,256]{1,0:T(8,128)(2,1)} %reduce-scatter.6.cloned.1.call-done), channel_id=1, source_target_pairs={{1,0},{2,1},{3,2},{4,3},{5,4},{6,5},{7,6},{8,7},{9,8},{10,9},{11,1... | collective-permute-start | bytes 196616 | tf_op jit(solution)/shard_map/ppermute | solution.py:17
  (91 other events, 126.7 us)
Sparse Core Ops, SparseCore 0:
  11.0 50.0 all-gather.5
  63.5 47.0 all-gather.7
  113.6 47.0 all-gather.3
  335.7 77.4 reduce-scatter.7
  417.0 77.2 reduce-scatter.5
  497.6 77.3 reduce-scatter.3
where the time goes:
time: 586 us; the launch traced here: 583 us
  waiting for transfers between devices  358 us (61%)
  matrix products  98.2 us (17%)
  local copies, waits for them, and re-layouts  58.3 us (10%)
  other arithmetic  42.7 us (7%)
  between operations  16.9 us (3%)
  starting transfers between devices  6.12 us (1%)
    reduce_scatter x1, waiting for transfers between devices, body(): lax.psum_scatter(grads_wide[0].astype(jnp.bfloat16), 'grp', scatter_dimen...  81.1 us
    reduce_scatter x1, waiting for transfers between devices, body(): lax.psum_scatter(grads_wide[1].astype(jnp.bfloat16), 'grp', scatter_dimen...  78.7 us
    reduce_scatter x1, waiting for transfers between devices, body(): lax.psum_scatter(grads_wide[2].astype(jnp.bfloat16), 'grp', scatter_dimen...  66.1 us
    all_gather x1, waiting for transfers between devices, body(): lax.all_gather(from_lower, 'grp', axis=0, tiled=True)  48 us
    dot_general x48, matrix products, masked_scores(): jnp.einsum('qd,kd->qk', query_head, key_head, preferred_element_type=jnp....  47.9 us
    all_gather x1, waiting for transfers between devices, body(): lax.all_gather(from_upper, 'grp', axis=0, tiled=True)  47.4 us
    while x208, local copies, waits for them, and re-layouts  31.5 us
    all_gather x1, waiting for transfers between devices, body(): lax.all_gather(paired, 'grp', axis=0, tiled=True)  29.8 us
  transfers between devices with their start and end apart: 10, of which 8 were waited for; matrix products, arithmetic and copies ran while one was open for 4% of the time, Pallas kernels for 0%

commit v1 on v0

v1 whole, which is shorter than its diff:
```python
import functools
import math

import jax
import jax.numpy as jnp
from jax import lax
from jax.experimental import pallas as pl
from jax.experimental.pallas import tpu as pltpu
from jax.sharding import PartitionSpec as P

HEAD = 128
ROWS = 128
WIDE = 512
NEG = -1e30
SCALE = 1.0 / math.sqrt(HEAD)
EXP2_SCALE = SCALE * math.log2(math.e)
F32 = jnp.float32
BF16 = jnp.bfloat16

AXIS_OF = (1, 0, 3, 2)


def dot(a, b):
    return jnp.dot(a, b, preferred_element_type=F32)


def kernel(
    q_ref, k_ref, v_ref, do_ref, order_ref,
    att_ref, gq_ref, gk_ref, gv_ref,
    k_own, v_own, k_far, v_far, k_sib, v_sib,
    q_in, do_in, q_t, q_n, do_t, do_n,
    s_far, s_sib, s_own, s_tri,
    w_far, w_sib, w_own, w_tri,
    top, total, out_t, dq_t, delta,
    acc_far, acc_own, g_sib, g_sib_in,
    red_out, red_in, far_out, far_in, o_out, dq_out,
    gat_send, gat_recv, sib_send, sib_recv, far_send, far_recv,
    tile_send, tile_recv, par_send, par_recv,
    gs_send, gs_recv, red_send, red_recv,
):
    grp = lax.axis_index("grp")
    blk = lax.axis_index("blk")
    y, x = lax.div(grp, 4), lax.rem(grp, 4)
    core = lax.rem(blk, 2)
    sib_blk = blk + 1 - 2 * core
    far_blk = lax.rem(blk + 15 + 2 * core, 16)
    side = lax.div(grp, 8)
    low = jnp.where(grp < 8, grp, 15 - grp)

    def flip(v):
        return v + 1 - 2 * lax.rem(v, 2)

    def near(grp_id):
        return {"grp": grp_id, "blk": blk}

    flips = (
        near(flip(y) * 4 + x),
        near((3 - y) * 4 + x),
        near(y * 4 + flip(x)),
        near(y * 4 + 3 - x),
    )
    partner = near(15 - grp)
    sibling = {"grp": grp, "blk": sib_blk}
    farther = {"grp": grp, "blk": far_blk}

    def place(grp_id):
        py, px = lax.div(grp_id, 4), lax.rem(grp_id, 4)
        return (
            lax.div(py, 2), lax.rem(lax.div(py + 1, 2), 2),
            lax.div(px, 2), lax.rem(lax.div(px + 1, 2), 2),
        )

    mine = place(grp)
    remote = functools.partial(
        pltpu.make_async_remote_copy, device_id_type=pl.DeviceIdType.MESH
    )

    def grid_slice(full, other=None):
        picks = []
        for axis in range(4):
            if axis in full:
                picks.append(pl.ds(0, 2))
            elif axis == other:
                picks.append(pl.ds(1 - mine[axis], 1))
            else:
                picks.append(pl.ds(mine[axis], 1))
        return tuple(picks)

    barrier = pltpu.get_barrier_semaphore()
    for dev in flips + (partner, sibling, farther):
        pl.semaphore_signal(barrier, inc=1, device_id=dev, device_id_type=pl.DeviceIdType.MESH)

    k_own[mine] = k_ref[...]
    v_own[mine] = v_ref[...]
    pl.semaphore_wait(barrier, 7)

    own_cols = pl.ds(pl.multiple_of(side * WIDE, WIDE), WIDE)
    other_cols = pl.ds(pl.multiple_of((1 - side) * WIDE, WIDE), WIDE)

    def gather_copy(quarter, step):
        ref = (k_own, v_own)[quarter // 2]
        rows = pl.ds(64 * (quarter % 2), 64)
        full = [AXIS_OF[(quarter + t) % 4] for t in range(step)]
        where = grid_slice(full) + (rows,)
        return remote(
            src_ref=ref.at[where], dst_ref=ref.at[where],
            send_sem=gat_send.at[quarter, step], recv_sem=gat_recv.at[quarter, step],
            device_id=flips[(quarter + step) % 4],
        )

    def pass_on(quarter, step, to_sib):
        own = (k_own, v_own)[quarter // 2]
        dest = ((k_sib, v_sib) if to_sib else (k_far, v_far))[quarter // 2]
        rows = pl.ds(64 * (quarter % 2), 64)
        full = [AXIS_OF[(quarter + t) % 4] for t in range(step)]
        where = grid_slice(full, AXIS_OF[(quarter + step) % 4]) + (rows,)
        sends, recvs = (sib_send, sib_recv) if to_sib else (far_send, far_recv)
        return remote(
            src_ref=own.at[where], dst_ref=dest.at[where],
            send_sem=sends.at[quarter, step], recv_sem=recvs.at[quarter, step],
            device_id=sibling if to_sib else farther,
        )

    def tile_copy(index):
        own = (k_own, v_own)[index // 2]
        dest = ((k_sib, v_sib), (k_far, v_far))[index % 2][index // 2]
        where = grid_slice(())
        return remote(
            src_ref=own.at[where], dst_ref=dest.at[where],
            send_sem=tile_send.at[index], recv_sem=tile_recv.at[index],
            device_id=(sibling, farther)[index % 2],
        )

    q_copy = remote(
        src_ref=q_ref.at[:, other_cols], dst_ref=q_in, send_sem=par_send.at[0],
        recv_sem=par_recv.at[0], device_id=partner,
    )
    do_copy = remote(
        src_ref=do_ref.at[:, other_cols], dst_ref=do_in, send_sem=par_send.at[1],
        recv_sem=par_recv.at[1], device_id=partner,
    )

    for quarter in range(4):
        gather_copy(quarter, 0).start()
    for index in range(4):
        tile_copy(index).start()
    q_copy.start()

    def spread(source, cols, index, flat, stacked):
        for head in range(4):
            part = source[:, pl.ds(pl.multiple_of(cols + head * HEAD, HEAD), HEAD)]
            flat[index, :, pl.ds(head * HEAD, HEAD)] = part.T
            if stacked is not None:
                stacked[index, pl.ds(head * HEAD, HEAD), :] = part

    spread(q_ref, side * WIDE, side, q_t, q_n)

    for step in range(4):
        for quarter in range(4):
            gather_copy(quarter, step).wait_recv()
            if step < 3:
                gather_copy(quarter, step + 1).start()
            pass_on(quarter, step, True).start()
            pass_on(quarter, step, False).start()
        if step == 0:
            spread(do_ref, side * WIDE, side, do_t, None)
        if step == 1:
            do_copy.start()
        if step == 2:
            q_copy.wait_recv()
            spread(q_in, 0, 1 - side, q_t, q_n)

    my_rank = order_ref[blk]
    sib_pick = jnp.where(order_ref[sib_blk] < my_rank, 0, 1)
    far_pick = jnp.where(order_ref[far_blk] < my_rank, 0, 1)

    def tiles(ref, half, i):
        return ref[half, lax.div(i, 2), lax.rem(i, 2)].reshape(2 * ROWS, HEAD)

    def fold_max(s):
        return jnp.max(s.reshape(-1, 8, WIDE), axis=0)

    def fold_sum(s):
        return jnp.sum(s.reshape(-1, 8, WIDE), axis=0)

    def tri_unit(u):
        first = u <= low
        which = jnp.where(first, 0, 1)
        tile = jnp.where(first, u, u + 7 - low)
        return which, place(tile), (u == low) | (u == 8)

    top[...] = jnp.full((2, 8, WIDE), NEG, F32)

    def own_scores(i, _):
        s = dot(tiles(k_own, 0, i), q_t[1])
        s_own[i] = s
        top[1] = jnp.maximum(top[1], fold_max(s))
        return 0

    def tri_scores(u, _):
        which, tile, diag = tri_unit(u)
        s = dot(k_own[tile], q_t[which])
        key_row = lax.broadcasted_iota(jnp.int32, (ROWS, WIDE), 0)
        query_row = lax.rem(lax.broadcasted_iota(jnp.int32, (ROWS, WIDE), 1), ROWS)
        limit = query_row + jnp.where(diag, 0, ROWS)
        s = jnp.where(key_row <= limit, s, NEG)
        s_tri[u] = s
        top[which] = jnp.maximum(top[which], fold_max(s))
        return 0

    def side_scores(keys, scores, pick):
        def step(i, _):
            s = dot(tiles(keys, 0, i), q_t[1])
            scores[0, i] = s
            top_up = jnp.maximum(top[1], fold_max(s))
            t = dot(tiles(keys, pick, i), q_t[pick])
            scores[1, i] = t
            peak = fold_max(t)
            top[0] = jnp.maximum(top[0], jnp.where(pick == 0, peak, NEG))
            top[1] = jnp.maximum(top_up, jnp.where(pick == 1, peak, NEG))
            return 0

        lax.fori_loop(0, 4, step, 0)

    lax.fori_loop(0, 4, own_scores, 0)
    lax.fori_loop(0, 9, tri_scores, 0)

    def wait_tiles(to_sib):
        for index in (0, 2) if to_sib else (1, 3):
            tile_copy(index).wait_recv()
        for step in range(4):
            for quarter in range(4):
                pass_on(quarter, step, to_sib).wait_recv()

    do_copy.wait_recv()
    spread(do_in, 0, 1 - side, do_t, None)
    wait_tiles(True)
    side_scores(k_sib, s_sib, sib_pick)
    wait_tiles(False)
    side_scores(k_far, s_far, far_pick)

    for s in range(2):
        top[s, pl.ds(0, 1)] = jnp.max(top[s], axis=0, keepdims=True) * EXP2_SCALE
    total[...] = jnp.zeros((2, 8, WIDE), F32)
    out_t[...] = jnp.zeros((2, HEAD, WIDE), F32)

    def weigh(s, peak):
        w = jnp.exp2(s * EXP2_SCALE - peak)
        return w.astype(BF16), fold_sum(w)

    def own_weights(i, _):
        w, add = weigh(s_own[i], top[1, pl.ds(0, 1)])
        w_own[i] = w
        total[1] += add
        out_t[1] += dot(tiles(v_own, 0, i).T, w)
        return 0

    def tri_weights(u, _):
        which, tile, _ = tri_unit(u)
        w, add = weigh(s_tri[u], top[which, pl.ds(0, 1)])
        w_tri[u] = w
        total[which] += add
        out_t[which] += dot(v_own[tile].T, w)
        return 0

    def side_weights(vals, scores, weights, pick):
        def step(i, _):
            w, add = weigh(scores[0, i], top[1, pl.ds(0, 1)])
            weights[0, i] = w
            part = dot(tiles(vals, 0, i).T, w)
            w2, add2 = weigh(scores[1, i], top[pick, pl.ds(0, 1)])
            weights[1, i] = w2
            part2 = dot(tiles(vals, pick, i).T, w2)
            total[0] += jnp.where(pick == 0, add2, 0.0)
            total[1] += add + jnp.where(pick == 1, add2, 0.0)
            out_t[0] += jnp.where(pick == 0, part2, 0.0)
            out_t[1] += part + jnp.where(pick == 1, part2, 0.0)
            return 0

        lax.fori_loop(0, 4, step, 0)

    lax.fori_loop(0, 4, own_weights, 0)
    lax.fori_loop(0, 9, tri_weights, 0)
    side_weights(v_sib, s_sib, w_sib, sib_pick)
    side_weights(v_far, s_far, w_far, far_pick)

    o_copy = remote(
        src_ref=o_out, dst_ref=att_ref.at[:, own_cols], send_sem=par_send.at[2],
        recv_sem=par_recv.at[2], device_id=partner,
    )
    dq_copy = remote(
        src_ref=dq_out, dst_ref=gq_ref.at[:, own_cols], send_sem=par_send.at[3],
        recv_sem=par_recv.at[3], device_id=partner,
    )

    def finish(index, dest, base):
        recip = 1.0 / jnp.sum(total[index], axis=0, keepdims=True)
        o = (out_t[index] * recip).astype(BF16)
        grads = do_t[index].astype(F32)
        delta[index] = jnp.sum(grads * o.astype(F32), axis=0, keepdims=True) * recip
        scaled = (grads * recip).astype(BF16)
        do_t[index] = scaled
        for head in range(4):
            cols = slice(head * HEAD, (head + 1) * HEAD)
            do_n[index, cols, :] = scaled[:, cols].T
            dest[:, pl.ds(pl.multiple_of(base + head * HEAD, HEAD), HEAD)] = o[:, cols].T

    finish(1 - side, o_out, 0)
    o_copy.start()
    finish(side, att_ref, side * WIDE)

    dq_t[...] = jnp.zeros((2, HEAD, WIDE), F32)

    def back(keys, vals, w, index):
        dp = dot(vals, do_t[index])
        ds = (w.astype(F32) * (dp - delta[index])).astype(BF16)
        dv = dot(w, do_n[index])
        dk = dot(ds, q_n[index]) * SCALE
        return dk, dv, dot(keys.T, ds)

    def reduce_part(acc, quarter, step, send):
        full = [AXIS_OF[(quarter + t) % 4] for t in range(step + 1, 4)]
        where = grid_slice(full, AXIS_OF[(quarter + step) % 4] if send else None)
        return (quarter // 2,) + where + (pl.ds(64 * (quarter % 2), 64),)

    OFFSET = (0, 8, 12, 14)

    def reduce_copy(which, quarter, step):
        span = pl.ds(OFFSET[step], 8 >> step)
        return remote(
            src_ref=red_out.at[which, quarter, span], dst_ref=red_in.at[which, quarter, span],
            send_sem=red_send.at[which, quarter, step], recv_sem=red_recv.at[which, quarter, step],
            device_id=flips[(quarter + step) % 4],
        )

    def reduce_send(which, acc, step):
        for quarter in range(4):
            part = acc[reduce_part(acc, quarter, step, True)]
            red_out[which, quarter, pl.ds(OFFSET[step], 8 >> step)] = part.reshape(
                8 >> step, 64, HEAD
            ).astype(BF16)
            reduce_copy(which, quarter, step).start()

    def reduce_take(which, acc, step):
        for quarter in range(4):
            reduce_copy(which, quarter, step).wait_recv()
            where = reduce_part(acc, quarter, step, False)
            part = acc[where]
            came = red_in[which, quarter, pl.ds(OFFSET[step], 8 >> step)]
            acc[where] = part + came.astype(F32).reshape(part.shape)

    def side_back(keys, vals, weights, pick, store):
        def step(i, _):
            dk, dv, dq = back(tiles(keys, 0, i), tiles(vals, 0, i), weights[0, i], 1)
            dk2, dv2, dq2 = back(tiles(keys, pick, i), tiles(vals, pick, i), weights[1, i], pick)
            dq_t[0] += jnp.where(pick == 0, dq2, 0.0)
            dq_t[1] += dq + jnp.where(pick == 1, dq2, 0.0)
            store(i, 0, 0, dk + jnp.where(pick == 0, dk2, 0.0))
            store(i, 1, 0, dv + jnp.where(pick == 0, dv2, 0.0))
            store(i, 0, 1, jnp.where(pick == 1, dk2, 0.0))
            store(i, 1, 1, jnp.where(pick == 1, dv2, 0.0))
            return 0

        lax.fori_loop(0, 4, step, 0)

    def far_store(i, kind, half, value):
        acc_far[kind, half, lax.div(i, 2), lax.rem(i, 2)] = value.reshape(2, ROWS, HEAD)

    def sib_copy(i, kind, half):
        where = (kind, half, lax.div(i, 2), lax.rem(i, 2))
        sem = (i * 2 + kind) * 2 + half
        return remote(
            src_ref=g_sib.at[where], dst_ref=g_sib_in.at[where],
            send_sem=gs_send.at[sem], recv_sem=gs_recv.at[sem], device_id=sibling,
        )

    def sib_store(i, kind, half, value):
        g_sib[kind, half, lax.div(i, 2), lax.rem(i, 2)] = value.reshape(2, ROWS, HEAD).astype(BF16)
        sib_copy(i, kind, half).start()

    side_back(k_far, v_far, w_far, far_pick, far_store)
    reduce_send(0, acc_far, 0)
    side_back(k_sib, v_sib, w_sib, sib_pick, sib_store)
    reduce_take(0, acc_far, 0)
    reduce_send(0, acc_far, 1)

    def own_back(i, _):
        dk, dv, dq = back(tiles(k_own, 0, i), tiles(v_own, 0, i), w_own[i], 1)
        where = (lax.div(i, 2), lax.rem(i, 2))
        acc_own[(0, 0) + where] = dk.reshape(2, ROWS, HEAD)
        acc_own[(1, 0) + where] = dv.reshape(2, ROWS, HEAD)
        dq_t[1] += dq
        return 0

    lax.fori_loop(0, 4, own_back, 0)
    acc_own[:, 1] = jnp.zeros((2, 2, 2, 2, ROWS, HEAD), F32)
    reduce_take(0, acc_far, 1)
    reduce_send(0, acc_far, 2)

    def tri_back(u, _):
        which, tile, _ = tri_unit(u)
        dk, dv, dq = back(k_own[tile], v_own[tile], w_tri[u], which)
        acc_own[(0,) + tile] += dk
        acc_own[(1,) + tile] += dv
        dq_t[which] += dq
        return 0

    lax.fori_loop(0, 9, tri_back, 0)

    reduce_take(0, acc_far, 2)
    reduce_send(0, acc_far, 3)

    def add_sib(i, _):
        for kind in range(2):
            for half in range(2):
                sib_copy(i, kind, half).wait_recv()
                where = (kind, half, lax.div(i, 2), lax.rem(i, 2))
                acc_own[where] += g_sib_in[where].astype(F32)
        return 0

    lax.fori_loop(0, 4, add_sib, 0)
    reduce_send(1, acc_own, 0)

    def finish_dq(index, dest, base):
        grads = (dq_t[index] * SCALE).astype(BF16)
        for head in range(4):
            cols = slice(head * HEAD, (head + 1) * HEAD)
            dest[:, pl.ds(pl.multiple_of(base + head * HEAD, HEAD), HEAD)] = grads[:, cols].T

    finish_dq(1 - side, dq_out, 0)
    dq_copy.start()
    reduce_take(0, acc_far, 3)
    for kind in range(2):
        far_out[kind] = acc_far[(kind,) + mine].astype(BF16)
    far_copy = remote(
        src_ref=far_out, dst_ref=far_in, send_sem=par_send.at[4],
        recv_sem=par_recv.at[4], device_id=farther,
    )
    far_copy.start()
    finish_dq(side, gq_ref, side * WIDE)

    reduce_take(1, acc_own, 0)
    for step in range(1, 4):
        reduce_send(1, acc_own, step)
        reduce_take(1, acc_own, step)
    far_copy.wait_recv()
    gk_ref[...] = (acc_own[(0,) + mine] + far_in[0].astype(F32)).astype(BF16)
    gv_ref[...] = (acc_own[(1,) + mine] + far_in[1].astype(F32)).astype(BF16)

    o_copy.wait_recv()
    dq_copy.wait_recv()
    for copy in (q_copy, do_copy, o_copy, dq_copy, far_copy):
        copy.wait_send()
    for index in range(4):
        tile_copy(index).wait_send()
    for step in range(4):
        for quarter in range(4):
            gather_copy(quarter, step).wait_send()
            pass_on(quarter, step, True).wait_send()
            pass_on(quarter, step, False).wait_send()
            reduce_copy(0, quarter, step).wait_send()
            reduce_copy(1, quarter, step).wait_send()

    def drain_sib(i, _):
        for kind in range(2):
            for half in range(2):
                sib_copy(i, kind, half).wait_send()
        return 0

    lax.fori_loop(0, 4, drain_sib, 0)


def body(queries, key_rows, values, out_grad, span_order):
    vmem = pl.BlockSpec(memory_space=pltpu.VMEM)
    kv = pltpu.VMEM((2, 2, 2, 2, ROWS, HEAD), BF16)
    dma = pltpu.SemaphoreType.DMA
    return pl.pallas_call(
        kernel,
        out_shape=(
            jax.ShapeDtypeStruct(queries.shape, BF16),
            jax.ShapeDtypeStruct(queries.shape, BF16),
            jax.ShapeDtypeStruct(key_rows.shape, BF16),
            jax.ShapeDtypeStruct(key_rows.shape, BF16),
        ),
        in_specs=[vmem] * 4 + [pl.BlockSpec(memory_space=pltpu.SMEM)],
        out_specs=(vmem,) * 4,
        scratch_shapes=[
            kv, kv, kv, kv, kv, kv,
            pltpu.VMEM((ROWS, WIDE), BF16), pltpu.VMEM((ROWS, WIDE), BF16),
            pltpu.VMEM((2, HEAD, WIDE), BF16), pltpu.VMEM((2, WIDE, HEAD), BF16),
            pltpu.VMEM((2, HEAD, WIDE), BF16), pltpu.VMEM((2, WIDE, HEAD), BF16),
            pltpu.VMEM((2, 4, 256, WIDE), F32), pltpu.VMEM((2, 4, 256, WIDE), F32),
            pltpu.VMEM((4, 256, WIDE), F32), pltpu.VMEM((9, ROWS, WIDE), F32),
            pltpu.VMEM((2, 4, 256, WIDE), BF16), pltpu.VMEM((2, 4, 256, WIDE), BF16),
            pltpu.VMEM((4, 256, WIDE), BF16), pltpu.VMEM((9, ROWS, WIDE), BF16),
            pltpu.VMEM((2, 8, WIDE), F32), pltpu.VMEM((2, 8, WIDE), F32),
            pltpu.VMEM((2, HEAD, WIDE), F32), pltpu.VMEM((2, HEAD, WIDE), F32),
            pltpu.VMEM((2, 1, WIDE), F32),
            pltpu.VMEM((2, 2, 2, 2, 2, ROWS, HEAD), F32),
            pltpu.VMEM((2, 2, 2, 2, 2, ROWS, HEAD), F32),
            pltpu.VMEM((2, 2, 2, 2, 2, ROWS, HEAD), BF16),
            pltpu.VMEM((2, 2, 2, 2, 2, ROWS, HEAD), BF16),
            pltpu.VMEM((2, 4, 15, 64, HEAD), BF16), pltpu.VMEM((2, 4, 15, 64, HEAD), BF16),
            pltpu.VMEM((2, ROWS, HEAD), BF16), pltpu.VMEM((2, ROWS, HEAD), BF16),
            pltpu.VMEM((ROWS, WIDE), BF16), pltpu.VMEM((ROWS, WIDE), BF16),
            dma((4, 4)), dma((4, 4)), dma((4, 4)), dma((4, 4)), dma((4, 4)), dma((4, 4)),
            dma((4,)), dma((4,)), dma((5,)), dma((5,)),
            dma((16,)), dma((16,)), dma((2, 4, 4)), dma((2, 4, 4)),
        ],
        compiler_params=pltpu.CompilerParams(
            collective_id=0, has_side_effects=True, vmem_limit_bytes=56 * 1024 * 1024
        ),
        cost_estimate=pl.CostEstimate(
            flops=5 * 10**9, bytes_accessed=2 * 10**6, transcendentals=3 * 10**6
        ),
    )(queries, key_rows, values, out_grad, span_order)


def solution(mesh):
    rows = P(("grp", "blk"), None)
    return jax.shard_map(
        body,
        mesh=mesh,
        in_specs=(rows, rows, rows, rows, P()),
        out_specs=(rows, rows, rows, rows),
        check_vma=False,
    )
```

time: 586 us -> 81.4 us (0.14)
  waiting for transfers between devices: 358 us -> 0 us
  matrix products: 98.2 us -> 0 us
  Pallas kernels: 0 us -> 76.6 us
  local copies, waits for them, and re-layouts: 58.3 us -> 3.86 us
  other arithmetic: 42.7 us -> 0 us
  between operations: 16.9 us -> 0.65 us
  starting transfers between devices: 6.12 us -> 0 us
    reduce_scatter x3 -> x0, waiting for transfers between devices: 226 us -> none  [the longest x1 81.1 us: body(): lax.psum_scatter(grads_wide[0].astype(jnp.bfloat16), 'grp', scatter_dimen...]
    all_gather x3 -> x0, waiting for transfers between devices: 125 us -> none  [the longest x1 48 us: body(): lax.all_gather(from_lower, 'grp', axis=0, tiled=True)]
    dot_general x168 -> x0, matrix products: 98.2 us -> none  [the longest x48 47.9 us: masked_scores(): jnp.einsum('qd,kd->qk', query_head, key_head, preferred_element_type=jnp....]
    pallas_call x0 -> x1, Pallas kernels: none -> 76.6 us  [body(): pl.pallas_call(kernel, out_shape=(jax.ShapeDtypeStruct(queries.shape, BF1...]
    while x212 -> x0, local copies, waits for them, and re-layouts: 37.2 us -> none
    add x26 -> x0, other arithmetic: 19.6 us -> none  [the longest x16 17.6 us: backward_step(): running[1 + member] + jnp.concatenate([key_grad, value_grad], axis=1)]
    slice x7 -> x0, local copies, waits for them, and re-layouts: 10.9 us -> none  [the longest x3 6.42 us: attend(): value_list = [member[:, head_dim:] for member in kv_sets]]
    reduce_sum x10 -> x0, other arithmetic: 8.74 us -> none  [the longest x8 6.12 us: forward_step(): row_total = row_total + jnp.sum(weights, axis=1, keepdims=True)]
  transfers between devices with their start and end apart: 10 -> 0, of which waited for: 8 -> 0; matrix products, arithmetic and copies ran while one was open for 4% -> 0% of each run, Pallas kernels for 0% -> 0%
where the time goes in v1:
time: 81.4 us; the launch traced here: 81.1 us
  Pallas kernels  76.6 us (94%)
  local copies, waits for them, and re-layouts  3.86 us (5%)
    pallas_call x1, Pallas kernels, body(): pl.pallas_call(kernel, out_shape=(jax.ShapeDtypeStruct(queries.shape, BF1...  76.6 us
    unnamed x10, local copies, waits for them, and re-layouts  3.86 us

profile of v1, /device:TPU:4, one launch (start us, length us, event | category | flops | bytes accessed | tf_op | source)
XLA Modules:
  0.0 81.1 jit_solution(17632238013813371836)
XLA Ops:
  0.6 76.6 %shard_map.84 = (bf16[128,1024]{1,0:T(8,128)(2,1)}, bf16[128,1024]{1,0:T(8,128)(2,1)}, bf16[128,128]{1,0:T(8,128)(2,1)}, bf16[128,128]{1,0:T(8,128)(2,1)}) custom-call(bf16[128,1024]{1,0:T(8,128)(2,1)} %q_ref.1, bf16[128,128]{1,0:T(8,128)(2,1)} %k_ref.1, bf16[128,128]{1,0:T(8,128)(2,1)} %v_ref.1, bf16[128,1024]{1,0:T(8,128)(2,1)} %do_ref.1, s32[16]{0:T(128)} %order_ref.1), custom_call_target="tpu_custom_call" | custom-call | flops 5000000000 | bytes 2000000 | tf_op jit(solution)/shard_map/pallas_call | solution.py:477
  77.3 0.0 copy-start
  77.3 1.7 %copy.13 = bf16[128,1024]{1,0:T(8,128)(2,1)} copy(bf16[128,1024]{1,0:T(8,128)(2,1)} %get-tuple-element.8) | data formatting | bytes 524288
  79.0 0.0 copy-done
  79.0 0.0 copy-start.2
  79.0 0.7 copy.14
  79.7 0.1 copy-done.2
  79.7 0.0 copy-start.1
  79.7 0.6 copy.15
  80.4 0.2 copy-done.1
  80.5 0.6 copy.16
Async XLA Ops:
  77.3 1.7 %copy-start = (bf16[128,1024]{1,0:T(8,128)(2,1)S(1)}, bf16[128,1024]{1,0:T(8,128)(2,1)}, u32[]{:S(2)}) copy-start(bf16[128,1024]{1,0:T(8,128)(2,1)} %get-tuple-element.9) | copy-start | bytes 786436
  79.0 0.8 copy-start.2
  79.7 0.8 copy-start.1

commit v2 on v1

v2 whole, which is shorter than its diff:
```python
import functools
import math

import jax
import jax.numpy as jnp
from jax import lax
from jax.experimental import pallas as pl
from jax.experimental.pallas import tpu as pltpu
from jax.sharding import PartitionSpec as P

HEAD = 128
ROWS = 128
WIDE = 512
NEG = -1e30
SCALE = 1.0 / math.sqrt(HEAD)
EXP2_SCALE = SCALE * math.log2(math.e)
F32 = jnp.float32
BF16 = jnp.bfloat16

WALK = (3, 0, 1, 2)
OFFSET = (0, 8, 12, 14)
FAR_V, OWN_V, FAR_K, OWN_K = range(4)
IS_OWN = (False, True, False, True)
KIND = (1, 1, 0, 0)


def dot(a, b):
    return jnp.dot(a, b, preferred_element_type=F32)


def dot_t(a, b):
    return lax.dot_general(a, b, (((1,), (1,)), ((), ())), preferred_element_type=F32)


def kernel(
    q_ref, k_ref, v_ref, do_ref, order_ref,
    att_ref, gq_ref, gk_ref, gv_ref,
    k_own, v_own, k_far, v_far, k_sib, v_sib,
    q_n, do_n,
    s_far, s_sib, s_own, w_far, w_sib, w_own,
    top, total, out_t, dq_t, delta,
    acc_far, acc_own, g_sib, g_sib_in,
    red_out, red_in, far_out, far_in, o_out, dq_out,
    gat_send, gat_recv, sib_send, sib_recv, far_send, far_recv,
    par_send, par_recv, gs_send, gs_recv, red_send, red_recv,
):
    grp = lax.axis_index("grp")
    blk = lax.axis_index("blk")
    y, x = lax.div(grp, 4), lax.rem(grp, 4)
    core = lax.rem(blk, 2)
    sib_blk = blk + 1 - 2 * core
    far_blk = lax.rem(blk + 15 + 2 * core, 16)
    side = lax.div(grp, 8)
    early_y = jnp.where(y < 2, y, 3 - y)
    span_tile = (early_y * 4 + x, (1 - early_y) * 4 + x)

    def flip(v):
        return v + 1 - 2 * lax.rem(v, 2)

    def near(grp_id):
        return {"grp": grp_id, "blk": blk}

    across = ((3 - y) * 4 + x, flip(y) * 4 + x, y * 4 + 3 - x, y * 4 + flip(x))
    partner = near(across[0])
    sibling = {"grp": grp, "blk": sib_blk}
    farther = {"grp": grp, "blk": far_blk}

    def place(grp_id):
        py, px = lax.div(grp_id, 4), lax.rem(grp_id, 4)
        return (
            lax.div(py, 2), lax.rem(lax.div(py + 1, 2), 2),
            lax.div(px, 2), lax.rem(lax.div(px + 1, 2), 2),
        )

    mine = place(grp)
    remote = functools.partial(
        pltpu.make_async_remote_copy, device_id_type=pl.DeviceIdType.MESH
    )

    barrier = pltpu.get_barrier_semaphore()
    for dev in tuple(near(a) for a in across) + (sibling, farther):
        pl.semaphore_signal(barrier, inc=1, device_id=dev, device_id_type=pl.DeviceIdType.MESH)

    k_own[mine] = k_ref[...]
    v_own[mine] = v_ref[...]
    own_cols = pl.ds(pl.multiple_of(side * WIDE, WIDE), WIDE)

    def stack(source, dest):
        for head in range(4):
            cols = pl.ds(pl.multiple_of(side * WIDE + head * HEAD, HEAD), HEAD)
            dest[side, pl.ds(head * HEAD, HEAD), :] = source[:, cols]

    pl.semaphore_wait(barrier, 6)

    def tile_at(mask):
        spot = []
        for axis in range(4):
            first = WALK.index(axis)
            on = (mask >> first) & 1
            on_back = (mask >> (3 - first)) & 1
            bit = mine[axis]
            if on == on_back:
                spot.append(1 - bit if on else bit)
            else:
                f = core if on_back else 1 - core
                spot.append(bit + f - 2 * bit * f)
        return tuple(spot)

    def toward(position):
        ahead, back = across[WALK[position]], across[WALK[3 - position]]
        return near(ahead + core * (back - ahead))

    own_kv, far_kv, sib_kv = (k_own, v_own), (k_far, v_far), (k_sib, v_sib)

    def hop(kind, mask, position, arriving):
        spot = tile_at(mask | (1 << position) if arriving else mask)
        return remote(
            src_ref=own_kv[kind].at[spot], dst_ref=own_kv[kind].at[spot],
            send_sem=gat_send.at[kind, position],
            recv_sem=gat_recv.at[kind, mask | (1 << position)],
            device_id=toward(position),
        )

    def hand_far(kind, mask):
        spot = tile_at(mask)
        return remote(
            src_ref=own_kv[kind].at[spot], dst_ref=far_kv[kind].at[spot],
            send_sem=far_send.at[kind], recv_sem=far_recv.at[kind], device_id=farther,
        )

    def far_all(kind):
        return remote(
            src_ref=own_kv[kind], dst_ref=far_kv[kind],
            send_sem=far_send.at[kind], recv_sem=far_recv.at[kind], device_id=farther,
        )

    def sib_all(kind):
        return remote(
            src_ref=own_kv[kind], dst_ref=sib_kv[kind],
            send_sem=sib_send.at[kind], recv_sem=sib_recv.at[kind], device_id=sibling,
        )

    def give_head(index, head):
        source, dest = ((q_ref, q_n), (do_ref, do_n))[index]
        cols = pl.ds(pl.multiple_of((1 - side) * WIDE + head * HEAD, HEAD), HEAD)
        return remote(
            src_ref=source.at[:, cols], dst_ref=dest.at[side, pl.ds(head * HEAD, HEAD)],
            send_sem=par_send.at[index], recv_sem=par_recv.at[index], device_id=partner,
        )

    def heads_all(index):
        dest = (q_n, do_n)[index].at[1 - side]
        return remote(
            src_ref=dest, dst_ref=dest,
            send_sem=par_send.at[index], recv_sem=par_recv.at[index], device_id=partner,
        )

    def relay(kind, mask):
        for position in range(mask.bit_length(), 4):
            hop(kind, mask, position, False).start()

    relay(0, 0)
    hand_far(0, 0).start()
    for head in range(4):
        give_head(0, head).start()
    relay(1, 0)
    stack(q_ref, q_n)
    stack(do_ref, do_n)
    late = [0]
    for level in range(1, 5):
        masks = [m for m in range(16) if bin(m).count("1") == level]
        for kind in range(2):
            for mask in masks:
                position = mask.bit_length() - 1
                hop(kind, mask - (1 << position), position, True).wait_recv()
                relay(kind, mask)
                if kind == 0:
                    hand_far(0, mask).start()
            if kind == 0:
                for mask in late:
                    hand_far(1, mask).start()
                if level == 4:
                    sib_all(0).start()
        late = masks
        if level == 3:
            for head in range(4):
                give_head(1, head).start()
    for mask in late:
        hand_far(1, mask).start()
    sib_all(1).start()

    my_rank = order_ref[blk]
    sib_pick = jnp.where(order_ref[sib_blk] < my_rank, 0, 1)
    far_pick = jnp.where(order_ref[far_blk] < my_rank, 0, 1)

    def half_of(ref, half):
        return ref[half].reshape(8 * ROWS, HEAD)

    def fold_max(s):
        return jnp.max(s.reshape(-1, 8, WIDE), axis=0)

    def fold_sum(s):
        return jnp.sum(s.reshape(-1, 8, WIDE), axis=0)

    def masked(s, half):
        row = lax.broadcasted_iota(jnp.int32, (ROWS, WIDE), 0)
        query = lax.rem(lax.broadcasted_iota(jnp.int32, (ROWS, WIDE), 1), ROWS)
        parts = []
        for tile in range(8):
            tile_y, tile_x = tile // 4, (0, 1, 3, 2)[tile % 4]
            rank = (1 - tile_y if half else tile_y) * 4 + tile_x
            seen = row <= query + (span_tile[half] - rank) * ROWS
            parts.append(jnp.where(seen, s[tile * ROWS : (tile + 1) * ROWS], NEG))
        return jnp.concatenate(parts, axis=0)

    top[...] = jnp.full((2, 8, WIDE), NEG, F32)

    def own_scores(job, half, which, mask):
        s = dot_t(half_of(k_own, half), q_n[which])
        if mask:
            s = masked(s, half)
        s_own[job] = s
        top[which] = jnp.maximum(top[which], fold_max(s))

    def side_scores(keys, scores, pick):
        s = dot_t(half_of(keys, 0), q_n[1])
        scores[0] = s
        top_up = jnp.maximum(top[1], fold_max(s))
        t = dot_t(half_of(keys, pick), q_n[pick])
        scores[1] = t
        peak = fold_max(t)
        top[0] = jnp.maximum(top[0], jnp.where(pick == 0, peak, NEG))
        top[1] = jnp.maximum(top_up, jnp.where(pick == 1, peak, NEG))

    heads_all(0).wait_recv()
    own_scores(0, 0, 1, False)
    own_scores(1, 0, 0, True)
    own_scores(2, 1, 1, True)
    sib_all(0).wait_recv()
    side_scores(k_sib, s_sib, sib_pick)
    far_all(0).wait_recv()
    side_scores(k_far, s_far, far_pick)

    for s in range(2):
        top[s, pl.ds(0, 1)] = jnp.max(top[s], axis=0, keepdims=True) * EXP2_SCALE
    total[...] = jnp.zeros((2, 8, WIDE), F32)
    out_t[...] = jnp.zeros((2, HEAD, WIDE), F32)

    def weigh(scores, weights, job, vals, half, which):
        peak = top[which, pl.ds(0, 1)]
        add = jnp.zeros((8, WIDE), F32)
        for i in range(4):
            rows = pl.ds(256 * i, 256)
            w = jnp.exp2(scores[job, rows] * EXP2_SCALE - peak)
            weights[job, rows] = w.astype(BF16)
            add = add + fold_sum(w)
        return add, dot(half_of(vals, half).T, weights[job])

    def own_weights(job, half, which):
        add, part = weigh(s_own, w_own, job, v_own, half, which)
        total[which] += add
        out_t[which] += part

    def side_weights(vals, scores, weights, pick):
        add, part = weigh(scores, weights, 0, vals, 0, 1)
        add2, part2 = weigh(scores, weights, 1, vals, pick, pick)
        total[0] += jnp.where(pick == 0, add2, 0.0)
        total[1] += add + jnp.where(pick == 1, add2, 0.0)
        out_t[0] += jnp.where(pick == 0, part2, 0.0)
        out_t[1] += part + jnp.where(pick == 1, part2, 0.0)

    own_weights(0, 0, 1)
    own_weights(1, 0, 0)
    own_weights(2, 1, 1)
    sib_all(1).wait_recv()
    side_weights(v_sib, s_sib, w_sib, sib_pick)
    far_all(1).wait_recv()
    side_weights(v_far, s_far, w_far, far_pick)

    o_copy = remote(
        src_ref=o_out, dst_ref=att_ref.at[:, own_cols], send_sem=par_send.at[2],
        recv_sem=par_recv.at[2], device_id=partner,
    )
    dq_copy = remote(
        src_ref=dq_out, dst_ref=gq_ref.at[:, own_cols], send_sem=par_send.at[3],
        recv_sem=par_recv.at[3], device_id=partner,
    )

    def finish(index, dest, base):
        recip = 1.0 / jnp.sum(total[index], axis=0, keepdims=True)
        for head in range(4):
            cols = slice(head * HEAD, (head + 1) * HEAD)
            recip_row = recip[:, cols]
            o = (out_t[index, :, pl.ds(head * HEAD, HEAD)] * recip_row).astype(BF16).T
            dest[:, pl.ds(pl.multiple_of(base + head * HEAD, HEAD), HEAD)] = o
            rows = pl.ds(head * HEAD, HEAD)
            grads = do_n[index, rows, :].astype(F32)
            along = jnp.sum(grads * o.astype(F32), axis=1, keepdims=True)
            along_row = jnp.broadcast_to(along, (ROWS, 8)).T[0:1]
            delta[index, :, pl.ds(head * HEAD, HEAD)] = along_row * recip_row
            recip_col = jnp.broadcast_to(recip_row, (8, ROWS)).T[:, 0:1]
            do_n[index, rows, :] = (grads * recip_col).astype(BF16)

    heads_all(1).wait_recv()
    finish(1 - side, o_out, 0)
    finish(side, att_ref, side * WIDE)

    def grid_slice(full, other=None):
        picks = []
        for axis in range(4):
            if axis in full:
                picks.append(pl.ds(0, 2))
            elif axis == other:
                picks.append(pl.ds(1 - mine[axis], 1))
            else:
                picks.append(pl.ds(mine[axis], 1))
        return tuple(picks)

    def reduce_part(family, quarter, step, send):
        full = [(quarter + t) % 4 for t in range(step + 1, 4)]
        where = grid_slice(full, (quarter + step) % 4 if send else None)
        return (KIND[family],) + where + (pl.ds(32 * quarter, 32),)

    def reduce_copy(family, quarter, step):
        span = pl.ds(OFFSET[step], 8 >> step)
        return remote(
            src_ref=red_out.at[family, quarter, span], dst_ref=red_in.at[family, quarter, span],
            send_sem=red_send.at[family, quarter, step],
            recv_sem=red_recv.at[family, quarter, step],
            device_id=near(across[(quarter + step) % 4]),
        )

    def held(family, where, step):
        part = (acc_own if IS_OWN[family] else acc_far)[where]
        if IS_OWN[family] and step == 0:
            part = part + g_sib_in[where].astype(F32)
        return part

    def reduce_send(family, step):
        for quarter in range(4):
            part = held(family, reduce_part(family, quarter, step, True), step)
            red_out[family, quarter, pl.ds(OFFSET[step], 8 >> step)] = part.reshape(
                8 >> step, 32, HEAD
            ).astype(BF16)
            reduce_copy(family, quarter, step).start()

    def reduce_take(family, step):
        acc = acc_own if IS_OWN[family] else acc_far
        for quarter in range(4):
            reduce_copy(family, quarter, step).wait_recv()
            where = reduce_part(family, quarter, step, False)
            part = held(family, where, step)
            came = red_in[family, quarter, pl.ds(OFFSET[step], 8 >> step)]
            acc[where] = part + came.astype(F32).reshape(part.shape)

    def reduce_next(family, step):
        reduce_take(family, step)
        reduce_send(family, step + 1)

    def far_copy(kind):
        return remote(
            src_ref=far_out.at[kind], dst_ref=far_in.at[kind], send_sem=par_send.at[4 + kind],
            recv_sem=par_recv.at[4 + kind], device_id=farther,
        )

    def far_finish(family):
        reduce_take(family, 3)
        kind = KIND[family]
        far_out[kind] = acc_far[(kind,) + mine].astype(BF16)
        far_copy(kind).start()

    def sib_copy(kind):
        return remote(
            src_ref=g_sib.at[kind], dst_ref=g_sib_in.at[kind],
            send_sem=gs_send.at[kind], recv_sem=gs_recv.at[kind], device_id=sibling,
        )

    def store(ref, kind, half, value):
        ref[kind, half] = value.reshape(2, 2, 2, ROWS, HEAD).astype(ref.dtype)

    def side_dv(weights, pick, ref):
        dv = dot(weights[0], do_n[1])
        dv2 = dot(weights[1], do_n[pick])
        store(ref, 1, 0, dv + jnp.where(pick == 0, dv2, 0.0))
        store(ref, 1, 1, jnp.where(pick == 1, dv2, 0.0))

    side_dv(w_far, far_pick, acc_far)
    reduce_send(FAR_V, 0)
    side_dv(w_sib, sib_pick, g_sib)
    sib_copy(1).start()
    o_copy.start()
    store(acc_own, 1, 0, dot(w_own[0], do_n[1]) + dot(w_own[1], do_n[0]))
    store(acc_own, 1, 1, dot(w_own[2], do_n[1]))
    sib_copy(1).wait_recv()
    reduce_send(OWN_V, 0)

    def back_dk(vals, half, weights, job, which):
        dp = dot_t(half_of(vals, half), do_n[which])
        ds = (weights[job].astype(F32) * (dp - delta[which])).astype(BF16)
        weights[job] = ds
        return dot(ds, q_n[which]) * SCALE

    def side_dk(vals, weights, pick, ref):
        dk = back_dk(vals, 0, weights, 0, 1)
        dk2 = back_dk(vals, pick, weights, 1, pick)
        store(ref, 0, 0, dk + jnp.where(pick == 0, dk2, 0.0))
        store(ref, 0, 1, jnp.where(pick == 1, dk2, 0.0))

    side_dk(v_far, w_far, far_pick, acc_far)
    reduce_next(FAR_V, 0)
    reduce_send(FAR_K, 0)
    side_dk(v_sib, w_sib, sib_pick, g_sib)
    sib_copy(0).start()
    reduce_next(OWN_V, 0)
    reduce_next(FAR_V, 1)
    store(acc_own, 0, 0, back_dk(v_own, 0, w_own, 0, 1) + back_dk(v_own, 0, w_own, 1, 0))
    reduce_next(FAR_K, 0)
    store(acc_own, 0, 1, back_dk(v_own, 1, w_own, 2, 1))
    sib_copy(0).wait_recv()
    reduce_send(OWN_K, 0)
    reduce_next(OWN_V, 1)
    reduce_next(FAR_V, 2)

    dq_t[...] = jnp.zeros((2, HEAD, WIDE), F32)

    def back_dq(keys, half, weights, job):
        return dot(half_of(keys, half).T, weights[job])

    def side_dq(keys, weights, pick):
        dq = back_dq(keys, 0, weights, 0)
        dq2 = back_dq(keys, pick, weights, 1)
        dq_t[0] += jnp.where(pick == 0, dq2, 0.0)
        dq_t[1] += dq + jnp.where(pick == 1, dq2, 0.0)

    side_dq(k_far, w_far, far_pick)
    reduce_next(FAR_K, 1)
    side_dq(k_sib, w_sib, sib_pick)
    reduce_next(OWN_K, 0)
    reduce_next(OWN_V, 2)
    far_finish(FAR_V)
    dq_t[0] += back_dq(k_own, 0, w_own, 1)
    dq_t[1] += back_dq(k_own, 0, w_own, 0) + back_dq(k_own, 1, w_own, 2)

    def finish_dq(index, dest, base):
        grads = (dq_t[index] * SCALE).astype(BF16)
        for head in range(4):
            cols = slice(head * HEAD, (head + 1) * HEAD)
            dest[:, pl.ds(pl.multiple_of(base + head * HEAD, HEAD), HEAD)] = grads[:, cols].T

    reduce_next(FAR_K, 2)
    finish_dq(1 - side, dq_out, 0)
    dq_copy.start()
    reduce_next(OWN_K, 1)
    finish_dq(side, gq_ref, side * WIDE)
    reduce_take(OWN_V, 3)
    far_finish(FAR_K)
    reduce_next(OWN_K, 2)
    far_copy(1).wait_recv()
    gv_ref[...] = (acc_own[(1,) + mine] + far_in[1].astype(F32)).astype(BF16)
    reduce_take(OWN_K, 3)
    far_copy(0).wait_recv()
    gk_ref[...] = (acc_own[(0,) + mine] + far_in[0].astype(F32)).astype(BF16)

    o_copy.wait_recv()
    dq_copy.wait_recv()
    for copy in (heads_all(0), heads_all(1), o_copy, dq_copy):
        copy.wait_send()
    for kind in range(2):
        far_copy(kind).wait_send()
        sib_copy(kind).wait_send()
        sib_all(kind).wait_send()
        far_all(kind).wait_send()
        for position in range(4):
            spans = tuple(
                pl.ds(0, 2 if axis >= 4 - position else 1) for axis in range(4)
            )
            part = own_kv[kind].at[spans]
            remote(
                src_ref=part, dst_ref=part, send_sem=gat_send.at[kind, position],
                recv_sem=gat_recv.at[kind, 0], device_id=toward(position),
            ).wait_send()
    for family in range(4):
        for step in range(4):
            for quarter in range(4):
                reduce_copy(family, quarter, step).wait_send()


def body(queries, key_rows, values, out_grad, span_order):
    vmem = pl.BlockSpec(memory_space=pltpu.VMEM)
    kv = pltpu.VMEM((2, 2, 2, 2, ROWS, HEAD), BF16)
    dma = pltpu.SemaphoreType.DMA
    return pl.pallas_call(
        kernel,
        out_shape=(
            jax.ShapeDtypeStruct(queries.shape, BF16),
            jax.ShapeDtypeStruct(queries.shape, BF16),
            jax.ShapeDtypeStruct(key_rows.shape, BF16),
            jax.ShapeDtypeStruct(key_rows.shape, BF16),
        ),
        in_specs=[vmem] * 4 + [pl.BlockSpec(memory_space=pltpu.SMEM)],
        out_specs=(vmem,) * 4,
        scratch_shapes=[
            kv, kv, kv, kv, kv, kv,
            pltpu.VMEM((2, WIDE, HEAD), BF16), pltpu.VMEM((2, WIDE, HEAD), BF16),
            pltpu.VMEM((2, 1024, WIDE), F32), pltpu.VMEM((2, 1024, WIDE), F32),
            pltpu.VMEM((3, 1024, WIDE), F32),
            pltpu.VMEM((2, 1024, WIDE), BF16), pltpu.VMEM((2, 1024, WIDE), BF16),
            pltpu.VMEM((3, 1024, WIDE), BF16),
            pltpu.VMEM((2, 8, WIDE), F32), pltpu.VMEM((2, 8, WIDE), F32),
            pltpu.VMEM((2, HEAD, WIDE), F32), pltpu.VMEM((2, HEAD, WIDE), F32),
            pltpu.VMEM((2, 1, WIDE), F32),
            pltpu.VMEM((2, 2, 2, 2, 2, ROWS, HEAD), F32),
            pltpu.VMEM((2, 2, 2, 2, 2, ROWS, HEAD), F32),
            pltpu.VMEM((2, 2, 2, 2, 2, ROWS, HEAD), BF16),
            pltpu.VMEM((2, 2, 2, 2, 2, ROWS, HEAD), BF16),
            pltpu.VMEM((4, 4, 15, 32, HEAD), BF16), pltpu.VMEM((4, 4, 15, 32, HEAD), BF16),
            pltpu.VMEM((2, ROWS, HEAD), BF16), pltpu.VMEM((2, ROWS, HEAD), BF16),
            pltpu.VMEM((ROWS, WIDE), BF16), pltpu.VMEM((ROWS, WIDE), BF16),
            dma((2, 4)), dma((2, 16)), dma((2,)), dma((2,)), dma((2,)), dma((2,)),
            dma((6,)), dma((6,)), dma((2,)), dma((2,)), dma((4, 4, 4)), dma((4, 4, 4)),
        ],
        compiler_params=pltpu.CompilerParams(
            collective_id=0, has_side_effects=True, vmem_limit_bytes=56 * 1024 * 1024
        ),
        cost_estimate=pl.CostEstimate(
            flops=5 * 10**9, bytes_accessed=2 * 10**6, transcendentals=3 * 10**6
        ),
    )(queries, key_rows, values, out_grad, span_order)


def solution(mesh):
    rows = P(("grp", "blk"), None)
    return jax.shard_map(
        body,
        mesh=mesh,
        in_specs=(rows, rows, rows, rows, P()),
        out_specs=(rows, rows, rows, rows),
        check_vma=False,
    )
```

time: 81.4 us -> 63.4 us (0.78); the launches traced: 81.1 us -> 62.3 us
  Pallas kernels: 76.6 us -> 57.8 us
    pallas_call x1, Pallas kernels: 76.6 us -> 57.8 us  [body(): pl.pallas_call(kernel, out_shape=(jax.ShapeDtypeStruct(queries.shape, BF1...]
where the time goes in v2:
time: 63.4 us; the launch traced here: 62.3 us
  Pallas kernels  57.8 us (91%)
  local copies, waits for them, and re-layouts  3.86 us (6%)
  between operations  0.65 us (1%)
    pallas_call x1, Pallas kernels, body(): pl.pallas_call(kernel, out_shape=(jax.ShapeDtypeStruct(queries.shape, BF1...  57.8 us
    unnamed x10, local copies, waits for them, and re-layouts  3.86 us

profile of v2, /device:TPU:4, one launch (start us, length us, event | category | flops | bytes accessed | tf_op | source)
XLA Modules:
  0.0 62.3 jit_solution(2913226292357819590)
XLA Ops:
  0.6 57.8 %shard_map.84 = (bf16[128,1024]{1,0:T(8,128)(2,1)}, bf16[128,1024]{1,0:T(8,128)(2,1)}, bf16[128,128]{1,0:T(8,128)(2,1)}, bf16[128,128]{1,0:T(8,128)(2,1)}) custom-call(bf16[128,1024]{1,0:T(8,128)(2,1)} %q_ref.1, bf16[128,128]{1,0:T(8,128)(2,1)} %k_ref.1, bf16[128,128]{1,0:T(8,128)(2,1)} %v_ref.1, bf16[128,1024]{1,0:T(8,128)(2,1)} %do_ref.1, s32[16]{0:T(128)} %order_ref.1), custom_call_target="tpu_custom_call" | custom-call | flops 5000000000 | bytes 2000000 | tf_op jit(solution)/shard_map/pallas_call | solution.py:492
  58.4 0.0 copy-start
  58.4 1.7 %copy.13 = bf16[128,1024]{1,0:T(8,128)(2,1)} copy(bf16[128,1024]{1,0:T(8,128)(2,1)} %get-tuple-element.8) | data formatting | bytes 524288
  60.1 0.0 copy-done
  60.1 0.0 copy-start.2
  60.1 0.7 %copy.14 = bf16[128,1024]{1,0:T(8,128)(2,1)} copy(bf16[128,1024]{1,0:T(8,128)(2,1)S(1)} %copy-done) | data formatting | bytes 524288
  60.8 0.1 copy-done.2
  60.9 0.0 copy-start.1
  60.9 0.6 copy.15
  61.5 0.2 copy-done.1
  61.7 0.6 copy.16
Async XLA Ops:
  58.4 1.7 %copy-start = (bf16[128,1024]{1,0:T(8,128)(2,1)S(1)}, bf16[128,1024]{1,0:T(8,128)(2,1)}, u32[]{:S(2)}) copy-start(bf16[128,1024]{1,0:T(8,128)(2,1)} %get-tuple-element.9) | copy-start | bytes 786436
  60.1 0.8 %copy-start.2 = (bf16[128,128]{1,0:T(8,128)(2,1)S(1)}, bf16[128,128]{1,0:T(8,128)(2,1)}, u32[]{:S(2)}) copy-start(bf16[128,128]{1,0:T(8,128)(2,1)} %get-tuple-element.10) | copy-start | bytes 98308
  60.9 0.8 %copy-start.1 = (bf16[128,128]{1,0:T(8,128)(2,1)S(1)}, bf16[128,128]{1,0:T(8,128)(2,1)}, u32[]{:S(2)}) copy-start(bf16[128,128]{1,0:T(8,128)(2,1)} %get-tuple-element.11) | copy-start | bytes 98308

commit v3 on v2

--- a/solution.py
+++ b/solution.py
@@ -17,7 +17,7 @@
 F32 = jnp.float32
 BF16 = jnp.bfloat16
 
-WALK = (3, 0, 1, 2)
+STEPS = (1, 3, 2)
 OFFSET = (0, 8, 12, 14)
 FAR_V, OWN_V, FAR_K, OWN_K = range(4)
 IS_OWN = (False, True, False, True)
@@ -60,6 +60,11 @@
     def near(grp_id):
         return {"grp": grp_id, "blk": blk}
 
+    def shifted(first, second):
+        step_x = first + core * (second - first)
+        step_y = second + core * (first - second)
+        return lax.rem(y + step_y, 4) * 4 + lax.rem(x + step_x, 4)
+
     across = ((3 - y) * 4 + x, flip(y) * 4 + x, y * 4 + 3 - x, y * 4 + flip(x))
     partner = near(across[0])
     sibling = {"grp": grp, "blk": sib_blk}
@@ -78,7 +83,8 @@
     )
 
     barrier = pltpu.get_barrier_semaphore()
-    for dev in tuple(near(a) for a in across) + (sibling, farther):
+    meet = tuple(near(shifted(s, 0)) for s in STEPS) + tuple(near(shifted(0, s)) for s in STEPS)
+    for dev in meet + (sibling, farther):
         pl.semaphore_signal(barrier, inc=1, device_id=dev, device_id_type=pl.DeviceIdType.MESH)
 
     k_own[mine] = k_ref[...]
@@ -90,39 +96,24 @@
             cols = pl.ds(pl.multiple_of(side * WIDE + head * HEAD, HEAD), HEAD)
             dest[side, pl.ds(head * HEAD, HEAD), :] = source[:, cols]
 
-    pl.semaphore_wait(barrier, 6)
-
-    def tile_at(mask):
-        spot = []
-        for axis in range(4):
-            first = WALK.index(axis)
-            on = (mask >> first) & 1
-            on_back = (mask >> (3 - first)) & 1
-            bit = mine[axis]
-            if on == on_back:
-                spot.append(1 - bit if on else bit)
-            else:
-                f = core if on_back else 1 - core
-                spot.append(bit + f - 2 * bit * f)
-        return tuple(spot)
-
-    def toward(position):
-        ahead, back = across[WALK[position]], across[WALK[3 - position]]
-        return near(ahead + core * (back - ahead))
+    pl.semaphore_wait(barrier, 8)
 
     own_kv, far_kv, sib_kv = (k_own, v_own), (k_far, v_far), (k_sib, v_sib)
 
-    def hop(kind, mask, position, arriving):
-        spot = tile_at(mask | (1 << position) if arriving else mask)
+    def spread(kind, first, second, arriving):
+        along_first = second == 0
+        if arriving:
+            spot = place(shifted((4 - first) % 4, (4 - second) % 4))
+        else:
+            spot = mine if along_first else place(shifted((4 - first) % 4, 0))
         return remote(
             src_ref=own_kv[kind].at[spot], dst_ref=own_kv[kind].at[spot],
-            send_sem=gat_send.at[kind, position],
-            recv_sem=gat_recv.at[kind, mask | (1 << position)],
-            device_id=toward(position),
-        )
-
-    def hand_far(kind, mask):
-        spot = tile_at(mask)
+            send_sem=gat_send.at[kind, first * 4 + second],
+            recv_sem=gat_recv.at[kind, first * 4 + second],
+            device_id=near(shifted(first, 0) if along_first else shifted(0, second)),
+        )
+
+    def hand_far(kind, spot):
         return remote(
             src_ref=own_kv[kind].at[spot], dst_ref=far_kv[kind].at[spot],
             send_sem=far_send.at[kind], recv_sem=far_recv.at[kind], device_id=farther,
@@ -155,39 +146,39 @@
             send_sem=par_send.at[index], recv_sem=par_recv.at[index], device_id=partner,
         )
 
-    def relay(kind, mask):
-        for position in range(mask.bit_length(), 4):
-            hop(kind, mask, position, False).start()
-
-    relay(0, 0)
-    hand_far(0, 0).start()
+    def begin(kind):
+        for step in reversed(STEPS):
+            spread(kind, step, 0, False).start()
+        for step in reversed(STEPS):
+            spread(kind, 0, step, False).start()
+
+    def arrive(kind, first, second):
+        spread(kind, first, second, True).wait_recv()
+        if second == 0:
+            for step in reversed(STEPS):
+                spread(kind, first, step, False).start()
+        hand_far(kind, place(shifted((4 - first) % 4, (4 - second) % 4))).start()
+
+    begin(0)
+    hand_far(0, mine).start()
     for head in range(4):
         give_head(0, head).start()
-    relay(1, 0)
+    begin(1)
     stack(q_ref, q_n)
     stack(do_ref, do_n)
-    late = [0]
-    for level in range(1, 5):
-        masks = [m for m in range(16) if bin(m).count("1") == level]
-        for kind in range(2):
-            for mask in masks:
-                position = mask.bit_length() - 1
-                hop(kind, mask - (1 << position), position, True).wait_recv()
-                relay(kind, mask)
-                if kind == 0:
-                    hand_far(0, mask).start()
-            if kind == 0:
-                for mask in late:
-                    hand_far(1, mask).start()
-                if level == 4:
-                    sib_all(0).start()
-        late = masks
-        if level == 3:
-            for head in range(4):
-                give_head(1, head).start()
-    for mask in late:
-        hand_far(1, mask).start()
-    sib_all(1).start()
+    for step in STEPS:
+        arrive(0, step, 0)
+    for step in STEPS:
+        arrive(0, 0, step)
+    hand_far(1, mine).start()
+    for step in STEPS:
+        arrive(1, step, 0)
+    for second in STEPS:
+        for first in STEPS:
+            arrive(0, first, second)
+    sib_all(0).start()
+    for head in range(4):
+        give_head(1, head).start()
 
     my_rank = order_ref[blk]
     sib_pick = jnp.where(order_ref[sib_blk] < my_rank, 0, 1)
@@ -234,8 +225,14 @@
 
     heads_all(0).wait_recv()
     own_scores(0, 0, 1, False)
+    for step in STEPS:
+        arrive(1, 0, step)
     own_scores(1, 0, 0, True)
     own_scores(2, 1, 1, True)
+    for second in STEPS:
+        for first in STEPS:
+            arrive(1, first, second)
+    sib_all(1).start()
     sib_all(0).wait_recv()
     side_scores(k_sib, s_sib, sib_pick)
     far_all(0).wait_recv()
@@ -384,16 +381,6 @@
         store(ref, 1, 0, dv + jnp.where(pick == 0, dv2, 0.0))
         store(ref, 1, 1, jnp.where(pick == 1, dv2, 0.0))
 
-    side_dv(w_far, far_pick, acc_far)
-    reduce_send(FAR_V, 0)
-    side_dv(w_sib, sib_pick, g_sib)
-    sib_copy(1).start()
-    o_copy.start()
-    store(acc_own, 1, 0, dot(w_own[0], do_n[1]) + dot(w_own[1], do_n[0]))
-    store(acc_own, 1, 1, dot(w_own[2], do_n[1]))
-    sib_copy(1).wait_recv()
-    reduce_send(OWN_V, 0)
-
     def back_dk(vals, half, weights, job, which):
         dp = dot_t(half_of(vals, half), do_n[which])
         ds = (weights[job].astype(F32) * (dp - delta[which])).astype(BF16)
@@ -406,20 +393,27 @@
         store(ref, 0, 0, dk + jnp.where(pick == 0, dk2, 0.0))
         store(ref, 0, 1, jnp.where(pick == 1, dk2, 0.0))
 
+    side_dv(w_far, far_pick, acc_far)
+    reduce_send(FAR_V, 0)
     side_dk(v_far, w_far, far_pick, acc_far)
-    reduce_next(FAR_V, 0)
     reduce_send(FAR_K, 0)
+    side_dv(w_sib, sib_pick, g_sib)
+    sib_copy(1).start()
+    o_copy.start()
     side_dk(v_sib, w_sib, sib_pick, g_sib)
     sib_copy(0).start()
-    reduce_next(OWN_V, 0)
-    reduce_next(FAR_V, 1)
+    reduce_next(FAR_V, 0)
+    store(acc_own, 1, 0, dot(w_own[0], do_n[1]) + dot(w_own[1], do_n[0]))
+    store(acc_own, 1, 1, dot(w_own[2], do_n[1]))
+    sib_copy(1).wait_recv()
+    reduce_send(OWN_V, 0)
+    reduce_next(FAR_K, 0)
     store(acc_own, 0, 0, back_dk(v_own, 0, w_own, 0, 1) + back_dk(v_own, 0, w_own, 1, 0))
-    reduce_next(FAR_K, 0)
     store(acc_own, 0, 1, back_dk(v_own, 1, w_own, 2, 1))
     sib_copy(0).wait_recv()
     reduce_send(OWN_K, 0)
-    reduce_next(OWN_V, 1)
-    reduce_next(FAR_V, 2)
+    reduce_next(FAR_V, 1)
+    reduce_next(FAR_K, 1)
 
     dq_t[...] = jnp.zeros((2, HEAD, WIDE), F32)
 
@@ -433,11 +427,11 @@
         dq_t[1] += dq + jnp.where(pick == 1, dq2, 0.0)
 
     side_dq(k_far, w_far, far_pick)
-    reduce_next(FAR_K, 1)
     side_dq(k_sib, w_sib, sib_pick)
+    reduce_next(OWN_V, 0)
     reduce_next(OWN_K, 0)
-    reduce_next(OWN_V, 2)
-    far_finish(FAR_V)
+    reduce_next(FAR_V, 2)
+    reduce_next(FAR_K, 2)
     dq_t[0] += back_dq(k_own, 0, w_own, 1)
     dq_t[1] += back_dq(k_own, 0, w_own, 0) + back_dq(k_own, 1, w_own, 2)
 
@@ -447,17 +441,19 @@
             cols = slice(head * HEAD, (head + 1) * HEAD)
             dest[:, pl.ds(pl.multiple_of(base + head * HEAD, HEAD), HEAD)] = grads[:, cols].T
 
-    reduce_next(FAR_K, 2)
+    reduce_next(OWN_V, 1)
+    reduce_next(OWN_K, 1)
     finish_dq(1 - side, dq_out, 0)
     dq_copy.start()
-    reduce_next(OWN_K, 1)
+    far_finish(FAR_V)
+    far_finish(FAR_K)
     finish_dq(side, gq_ref, side * WIDE)
+    reduce_next(OWN_V, 2)
+    reduce_next(OWN_K, 2)
     reduce_take(OWN_V, 3)
-    far_finish(FAR_K)
-    reduce_next(OWN_K, 2)
+    reduce_take(OWN_K, 3)
     far_copy(1).wait_recv()
     gv_ref[...] = (acc_own[(1,) + mine] + far_in[1].astype(F32)).astype(BF16)
-    reduce_take(OWN_K, 3)
     far_copy(0).wait_recv()
     gk_ref[...] = (acc_own[(0,) + mine] + far_in[0].astype(F32)).astype(BF16)
 
@@ -470,26 +466,26 @@
         sib_copy(kind).wait_send()
         sib_all(kind).wait_send()
         far_all(kind).wait_send()
-        for position in range(4):
-            spans = tuple(
-                pl.ds(0, 2 if axis >= 4 - position else 1) for axis in range(4)
-            )
-            part = own_kv[kind].at[spans]
-            remote(
-                src_ref=part, dst_ref=part, send_sem=gat_send.at[kind, position],
-                recv_sem=gat_recv.at[kind, 0], device_id=toward(position),
-            ).wait_send()
+        for first in range(4):
+            for second in range(4):
+                if first + second:
+                    spread(kind, first, second, False).wait_send()
     for family in range(4):
         for step in range(4):
             for quarter in range(4):
                 reduce_copy(family, quarter, step).wait_send()
 
 
+def hand_out(*refs):
+    for source, dest in zip(refs[:4], refs[4:]):
+        dest[...] = source[...]
+
+
 def body(queries, key_rows, values, out_grad, span_order):
     vmem = pl.BlockSpec(memory_space=pltpu.VMEM)
     kv = pltpu.VMEM((2, 2, 2, 2, ROWS, HEAD), BF16)
     dma = pltpu.SemaphoreType.DMA
-    return pl.pallas_call(
+    results = pl.pallas_call(
         kernel,
         out_shape=(
             jax.ShapeDtypeStruct(queries.shape, BF16),
@@ -516,7 +512,7 @@
             pltpu.VMEM((4, 4, 15, 32, HEAD), BF16), pltpu.VMEM((4, 4, 15, 32, HEAD), BF16),
             pltpu.VMEM((2, ROWS, HEAD), BF16), pltpu.VMEM((2, ROWS, HEAD), BF16),
             pltpu.VMEM((ROWS, WIDE), BF16), pltpu.VMEM((ROWS, WIDE), BF16),
-            dma((2, 4)), dma((2, 16)), dma((2,)), dma((2,)), dma((2,)), dma((2,)),
+            dma((2, 16)), dma((2, 16)), dma((2,)), dma((2,)), dma((2,)), dma((2,)),
             dma((6,)), dma((6,)), dma((2,)), dma((2,)), dma((4, 4, 4)), dma((4, 4, 4)),
         ],
         compiler_params=pltpu.CompilerParams(
@@ -526,6 +522,12 @@
             flops=5 * 10**9, bytes_accessed=2 * 10**6, transcendentals=3 * 10**6
         ),
     )(queries, key_rows, values, out_grad, span_order)
+    return pl.pallas_call(
+        hand_out,
+        out_shape=tuple(jax.ShapeDtypeStruct(r.shape, r.dtype) for r in results),
+        in_specs=[vmem] * 4,
+        out_specs=(vmem,) * 4,
+    )(*results)
 
 
 def solution(mesh):

time: 63.4 us -> 58.3 us (0.920)
  local copies, waits for them, and re-layouts: 3.86 us -> 0 us
  Pallas kernels: 57.8 us -> 57 us
    unnamed x10 -> x0, local copies, waits for them, and re-layouts: 3.86 us -> none
    pallas_call x1, Pallas kernels: 57.8 us -> 55.1 us  [body(): pl.pallas_call(kernel, out_shape=(jax.ShapeDtypeStruct(queries.shape, BF1...]
    pallas_call x0 -> x1, Pallas kernels: none -> 1.85 us  [body(): pl.pallas_call(hand_out, out_shape=tuple((jax.ShapeDtypeStruct(r.shape, r...]
where the time goes in v3:
time: 58.3 us; the launch traced here: 57.6 us
  Pallas kernels  57 us (98%)
  between operations  0.64 us (1%)
    pallas_call x1, Pallas kernels, body(): pl.pallas_call(kernel, out_shape=(jax.ShapeDtypeStruct(queries.shape, BF1...  55.1 us
    pallas_call x1, Pallas kernels, body(): pl.pallas_call(hand_out, out_shape=tuple((jax.ShapeDtypeStruct(r.shape, r...  1.85 us

profile of v3, /device:TPU:4, one launch (start us, length us, event | category | flops | bytes accessed | tf_op | source)
XLA Modules:
  0.0 57.6 jit_solution(8075154869486981245)
XLA Ops:
  0.6 55.1 %shard_map.84 = (bf16[128,1024]{1,0:T(8,128)(2,1)}, bf16[128,1024]{1,0:T(8,128)(2,1)}, bf16[128,128]{1,0:T(8,128)(2,1)}, bf16[128,128]{1,0:T(8,128)(2,1)}) custom-call(bf16[128,1024]{1,0:T(8,128)(2,1)} %q_ref.1, bf16[128,128]{1,0:T(8,128)(2,1)} %k_ref.1, bf16[128,128]{1,0:T(8,128)(2,1)} %v_ref.1, bf16[128,1024]{1,0:T(8,128)(2,1)} %do_ref.1, s32[16]{0:T(128)} %order_ref.1), custom_call_target="tpu_custom_call" | custom-call | flops 5000000000 | bytes 2000000 | tf_op jit(solution)/shard_map/pallas_call | solution.py:488
  55.8 1.9 %shard_map.85 = (bf16[128,1024]{1,0:T(8,128)(2,1)}, bf16[128,1024]{1,0:T(8,128)(2,1)}, bf16[128,128]{1,0:T(8,128)(2,1)}, bf16[128,128]{1,0:T(8,128)(2,1)}) custom-call(bf16[128,1024]{1,0:T(8,128)(2,1)} %get-tuple-element.8.refs_0_, bf16[128,1024]{1,0:T(8,128)(2,1)} %get-tuple-element.9.refs_1_, bf16[128,128]{1,0:T(8,128)(2,1)} %get-tuple-element.10.refs_2_, ...), custom_call_target="tpu_custom_call" | custom-call | tf_op jit(solution)/shard_map/pallas_call | solution.py:525

commit v4 on v3

--- a/solution.py
+++ b/solution.py
@@ -18,7 +18,6 @@
 BF16 = jnp.bfloat16
 
 STEPS = (1, 3, 2)
-OFFSET = (0, 8, 12, 14)
 FAR_V, OWN_V, FAR_K, OWN_K = range(4)
 IS_OWN = (False, True, False, True)
 KIND = (1, 1, 0, 0)
@@ -302,57 +301,62 @@
     finish(1 - side, o_out, 0)
     finish(side, att_ref, side * WIDE)
 
-    def grid_slice(full, other=None):
-        picks = []
-        for axis in range(4):
-            if axis in full:
-                picks.append(pl.ds(0, 2))
-            elif axis == other:
-                picks.append(pl.ds(1 - mine[axis], 1))
-            else:
-                picks.append(pl.ds(mine[axis], 1))
-        return tuple(picks)
-
-    def reduce_part(family, quarter, step, send):
-        full = [(quarter + t) % 4 for t in range(step + 1, 4)]
-        where = grid_slice(full, (quarter + step) % 4 if send else None)
-        return (KIND[family],) + where + (pl.ds(32 * quarter, 32),)
-
-    def reduce_copy(family, quarter, step):
-        span = pl.ds(OFFSET[step], 8 >> step)
-        return remote(
-            src_ref=red_out.at[family, quarter, span], dst_ref=red_in.at[family, quarter, span],
-            send_sem=red_send.at[family, quarter, step],
-            recv_sem=red_recv.at[family, quarter, step],
-            device_id=near(across[(quarter + step) % 4]),
-        )
-
-    def held(family, where, step):
+    def along(first_x, step):
+        return lax.rem(x + step, 4) if first_x else lax.rem(y + step, 4)
+
+    def line(v):
+        return (pl.ds(lax.div(v, 2), 1), pl.ds(lax.rem(lax.div(v + 1, 2), 2), 1))
+
+    def reduce_part(family, half, phase, step):
+        every = (pl.ds(0, 2), pl.ds(0, 2))
+        if phase == 0:
+            spot = line(along(half == 0, step))
+            where = every + spot if half == 0 else spot + every
+        else:
+            spot = line(along(half == 1, step))
+            where = spot + line(x) if half == 0 else line(y) + spot
+        return (KIND[family],) + where + (pl.ds(64 * half, 64),)
+
+    def slot(phase, step):
+        return pl.ds(4 * (step - 1), 4) if phase == 0 else pl.ds(11 + step, 1)
+
+    def reduce_copy(family, half, phase, step):
+        target = along((half == 0) == (phase == 0), step)
+        index = 3 * phase + step - 1
+        return remote(
+            src_ref=red_out.at[family, half, slot(phase, step)],
+            dst_ref=red_in.at[family, half, slot(phase, step)],
+            send_sem=red_send.at[family, half, index], recv_sem=red_recv.at[family, half, index],
+            device_id=near(y * 4 + target if (half == 0) == (phase == 0) else target * 4 + x),
+        )
+
+    def held(family, where, phase):
         part = (acc_own if IS_OWN[family] else acc_far)[where]
-        if IS_OWN[family] and step == 0:
+        if IS_OWN[family] and phase == 0:
             part = part + g_sib_in[where].astype(F32)
         return part
 
-    def reduce_send(family, step):
-        for quarter in range(4):
-            part = held(family, reduce_part(family, quarter, step, True), step)
-            red_out[family, quarter, pl.ds(OFFSET[step], 8 >> step)] = part.reshape(
-                8 >> step, 32, HEAD
-            ).astype(BF16)
-            reduce_copy(family, quarter, step).start()
-
-    def reduce_take(family, step):
+    def reduce_send(family, phase):
+        for step in (2, 1, 3):
+            for half in range(2):
+                part = held(family, reduce_part(family, half, phase, step), phase)
+                red_out[family, half, slot(phase, step)] = part.reshape(-1, 64, HEAD).astype(BF16)
+                reduce_copy(family, half, phase, step).start()
+
+    def reduce_take(family, phase):
         acc = acc_own if IS_OWN[family] else acc_far
-        for quarter in range(4):
-            reduce_copy(family, quarter, step).wait_recv()
-            where = reduce_part(family, quarter, step, False)
-            part = held(family, where, step)
-            came = red_in[family, quarter, pl.ds(OFFSET[step], 8 >> step)]
-            acc[where] = part + came.astype(F32).reshape(part.shape)
-
-    def reduce_next(family, step):
-        reduce_take(family, step)
-        reduce_send(family, step + 1)
+        for half in range(2):
+            where = reduce_part(family, half, phase, 0)
+            part = held(family, where, phase)
+            for step in (1, 3, 2):
+                reduce_copy(family, half, phase, step).wait_recv()
+                came = red_in[family, half, slot(phase, step)]
+                part = part + came.astype(F32).reshape(part.shape)
+            acc[where] = part
+
+    def reduce_next(family):
+        reduce_take(family, 0)
+        reduce_send(family, 1)
 
     def far_copy(kind):
         return remote(
@@ -361,7 +365,7 @@
         )
 
     def far_finish(family):
-        reduce_take(family, 3)
+        reduce_take(family, 1)
         kind = KIND[family]
         far_out[kind] = acc_far[(kind,) + mine].astype(BF16)
         far_copy(kind).start()
@@ -402,18 +406,16 @@
     o_copy.start()
     side_dk(v_sib, w_sib, sib_pick, g_sib)
     sib_copy(0).start()
-    reduce_next(FAR_V, 0)
+    reduce_next(FAR_V)
     store(acc_own, 1, 0, dot(w_own[0], do_n[1]) + dot(w_own[1], do_n[0]))
     store(acc_own, 1, 1, dot(w_own[2], do_n[1]))
     sib_copy(1).wait_recv()
     reduce_send(OWN_V, 0)
-    reduce_next(FAR_K, 0)
     store(acc_own, 0, 0, back_dk(v_own, 0, w_own, 0, 1) + back_dk(v_own, 0, w_own, 1, 0))
     store(acc_own, 0, 1, back_dk(v_own, 1, w_own, 2, 1))
     sib_copy(0).wait_recv()
     reduce_send(OWN_K, 0)
-    reduce_next(FAR_V, 1)
-    reduce_next(FAR_K, 1)
+    reduce_next(FAR_K)
 
     dq_t[...] = jnp.zeros((2, HEAD, WIDE), F32)
 
@@ -428,10 +430,8 @@
 
     side_dq(k_far, w_far, far_pick)
     side_dq(k_sib, w_sib, sib_pick)
-    reduce_next(OWN_V, 0)
-    reduce_next(OWN_K, 0)
-    reduce_next(FAR_V, 2)
-    reduce_next(FAR_K, 2)
+    far_finish(FAR_V)
+    reduce_next(OWN_V)
     dq_t[0] += back_dq(k_own, 0, w_own, 1)
     dq_t[1] += back_dq(k_own, 0, w_own, 0) + back_dq(k_own, 1, w_own, 2)
 
@@ -441,17 +441,13 @@
             cols = slice(head * HEAD, (head + 1) * HEAD)
             dest[:, pl.ds(pl.multiple_of(base + head * HEAD, HEAD), HEAD)] = grads[:, cols].T
 
-    reduce_next(OWN_V, 1)
-    reduce_next(OWN_K, 1)
     finish_dq(1 - side, dq_out, 0)
     dq_copy.start()
-    far_finish(FAR_V)
     far_finish(FAR_K)
+    reduce_next(OWN_K)
     finish_dq(side, gq_ref, side * WIDE)
-    reduce_next(OWN_V, 2)
-    reduce_next(OWN_K, 2)
-    reduce_take(OWN_V, 3)
-    reduce_take(OWN_K, 3)
+    reduce_take(OWN_V, 1)
+    reduce_take(OWN_K, 1)
     far_copy(1).wait_recv()
     gv_ref[...] = (acc_own[(1,) + mine] + far_in[1].astype(F32)).astype(BF16)
     far_copy(0).wait_recv()
@@ -471,9 +467,10 @@
                 if first + second:
                     spread(kind, first, second, False).wait_send()
     for family in range(4):
-        for step in range(4):
-            for quarter in range(4):
-                reduce_copy(family, quarter, step).wait_send()
+        for half in range(2):
+            for phase in range(2):
+                for step in STEPS:
+                    reduce_copy(family, half, phase, step).wait_send()
 
 
 def hand_out(*refs):
@@ -509,11 +506,11 @@
             pltpu.VMEM((2, 2, 2, 2, 2, ROWS, HEAD), F32),
             pltpu.VMEM((2, 2, 2, 2, 2, ROWS, HEAD), BF16),
             pltpu.VMEM((2, 2, 2, 2, 2, ROWS, HEAD), BF16),
-            pltpu.VMEM((4, 4, 15, 32, HEAD), BF16), pltpu.VMEM((4, 4, 15, 32, HEAD), BF16),
+            pltpu.VMEM((4, 2, 15, 64, HEAD), BF16), pltpu.VMEM((4, 2, 15, 64, HEAD), BF16),
             pltpu.VMEM((2, ROWS, HEAD), BF16), pltpu.VMEM((2, ROWS, HEAD), BF16),
             pltpu.VMEM((ROWS, WIDE), BF16), pltpu.VMEM((ROWS, WIDE), BF16),
             dma((2, 16)), dma((2, 16)), dma((2,)), dma((2,)), dma((2,)), dma((2,)),
-            dma((6,)), dma((6,)), dma((2,)), dma((2,)), dma((4, 4, 4)), dma((4, 4, 4)),
+            dma((6,)), dma((6,)), dma((2,)), dma((2,)), dma((4, 2, 6)), dma((4, 2, 6)),
         ],
         compiler_params=pltpu.CompilerParams(
             collective_id=0, has_side_effects=True, vmem_limit_bytes=56 * 1024 * 1024

time: 58.3 us -> 56.2 us (0.964)
  Pallas kernels: 57 us -> 55.1 us
    pallas_call x1, Pallas kernels: 55.1 us -> 53.3 us  [body(): pl.pallas_call(kernel, out_shape=(jax.ShapeDtypeStruct(queries.shape, BF1...]
where the time goes in v4:
time: 56.2 us; the launch traced here: 55.8 us
  Pallas kernels  55.1 us (98%)
  between operations  0.64 us (1%)
    pallas_call x1, Pallas kernels, body(): pl.pallas_call(kernel, out_shape=(jax.ShapeDtypeStruct(queries.shape, BF1...  53.3 us
    pallas_call x1, Pallas kernels, body(): pl.pallas_call(hand_out, out_shape=tuple((jax.ShapeDtypeStruct(r.shape, r...  1.85 us

profile of v4, /device:TPU:4, one launch (start us, length us, event | category | flops | bytes accessed | tf_op | source)
XLA Modules:
  0.0 55.8 jit_solution(11919003037477502200)
XLA Ops:
  0.6 53.3 %shard_map.84 = (bf16[128,1024]{1,0:T(8,128)(2,1)}, bf16[128,1024]{1,0:T(8,128)(2,1)}, bf16[128,128]{1,0:T(8,128)(2,1)}, bf16[128,128]{1,0:T(8,128)(2,1)}) custom-call(bf16[128,1024]{1,0:T(8,128)(2,1)} %q_ref.1, bf16[128,128]{1,0:T(8,128)(2,1)} %k_ref.1, bf16[128,128]{1,0:T(8,128)(2,1)} %v_ref.1, bf16[128,1024]{1,0:T(8,128)(2,1)} %do_ref.1, s32[16]{0:T(128)} %order_ref.1), custom_call_target="tpu_custom_call" | custom-call | flops 5000000000 | bytes 2000000 | tf_op jit(solution)/shard_map/pallas_call | solution.py:485
  53.9 1.9 %shard_map.85 = (bf16[128,1024]{1,0:T(8,128)(2,1)}, bf16[128,1024]{1,0:T(8,128)(2,1)}, bf16[128,128]{1,0:T(8,128)(2,1)}, bf16[128,128]{1,0:T(8,128)(2,1)}) custom-call(bf16[128,1024]{1,0:T(8,128)(2,1)} %get-tuple-element.8.refs_0_, bf16[128,1024]{1,0:T(8,128)(2,1)} %get-tuple-element.9.refs_1_, bf16[128,128]{1,0:T(8,128)(2,1)} %get-tuple-element.10.refs_2_, ...), custom_call_target="tpu_custom_call" | custom-call | tf_op jit(solution)/shard_map/pallas_call | solution.py:522

commit v5 on v4

--- a/solution.py
+++ b/solution.py
@@ -430,10 +430,10 @@
 
     side_dq(k_far, w_far, far_pick)
     side_dq(k_sib, w_sib, sib_pick)
-    far_finish(FAR_V)
-    reduce_next(OWN_V)
     dq_t[0] += back_dq(k_own, 0, w_own, 1)
     dq_t[1] += back_dq(k_own, 0, w_own, 0) + back_dq(k_own, 1, w_own, 2)
+    reduce_next(OWN_V)
+    far_finish(FAR_V)
 
     def finish_dq(index, dest, base):
         grads = (dq_t[index] * SCALE).astype(BF16)

time: 56.2 us -> 55.7 us (level)
  no operation moved by 1% of the time
where the time goes in v5:
time: 55.7 us; the launch traced here: 55.3 us
  Pallas kernels  54.6 us (98%)
  between operations  0.64 us (1%)
    pallas_call x1, Pallas kernels, body(): pl.pallas_call(kernel, out_shape=(jax.ShapeDtypeStruct(queries.shape, BF1...  52.8 us
    pallas_call x1, Pallas kernels, body(): pl.pallas_call(hand_out, out_shape=tuple((jax.ShapeDtypeStruct(r.shape, r...  1.85 us

profile of v5, /device:TPU:4, one launch (start us, length us, event | category | flops | bytes accessed | tf_op | source)
XLA Modules:
  0.0 55.3 jit_solution(14677576673199647155)
XLA Ops:
  0.6 52.8 %shard_map.84 = (bf16[128,1024]{1,0:T(8,128)(2,1)}, bf16[128,1024]{1,0:T(8,128)(2,1)}, bf16[128,128]{1,0:T(8,128)(2,1)}, bf16[128,128]{1,0:T(8,128)(2,1)}) custom-call(bf16[128,1024]{1,0:T(8,128)(2,1)} %q_ref.1, bf16[128,128]{1,0:T(8,128)(2,1)} %k_ref.1, bf16[128,128]{1,0:T(8,128)(2,1)} %v_ref.1, bf16[128,1024]{1,0:T(8,128)(2,1)} %do_ref.1, s32[16]{0:T(128)} %order_ref.1), custom_call_target="tpu_custom_call" | custom-call | flops 5000000000 | bytes 2000000 | tf_op jit(solution)/shard_map/pallas_call | solution.py:485
  53.4 1.9 %shard_map.85 = (bf16[128,1024]{1,0:T(8,128)(2,1)}, bf16[128,1024]{1,0:T(8,128)(2,1)}, bf16[128,128]{1,0:T(8,128)(2,1)}, bf16[128,128]{1,0:T(8,128)(2,1)}) custom-call(bf16[128,1024]{1,0:T(8,128)(2,1)} %get-tuple-element.8.refs_0_, bf16[128,1024]{1,0:T(8,128)(2,1)} %get-tuple-element.9.refs_1_, bf16[128,128]{1,0:T(8,128)(2,1)} %get-tuple-element.10.refs_2_, ...), custom_call_target="tpu_custom_call" | custom-call | tf_op jit(solution)/shard_map/pallas_call | solution.py:522
